TPU v7x, 32 devices: a whole 2x2x4 slice. The times are simulated.
32 devices in a mesh: dp: 2 (over x), fsdp: 16 (over z, y, core).
Axes of the slice: x: 2, y: 2, z: 4, core: 2. Of those that a mesh axis runs over, the one named last changes fastest.
Arguments:
- source: bfloat16 [8192, 512], P(('dp', 'fsdp')), may hold values from -6 to 6
- first_in: bfloat16 [8192, 512], P(('dp', 'fsdp')), may hold values from -6 to 6
- second_in: bfloat16 [8192, 512], P(('dp', 'fsdp')), may hold values from -6 to 6
- cot_first: bfloat16 [8192, 512], P(('dp', 'fsdp')), may hold values from -6 to 6
- cot_second: bfloat16 [8192, 512], P(('dp', 'fsdp')), may hold values from -6 to 6
- src_lengths: int32 [32, 8], P(('dp', 'fsdp')), may hold values from 1 to 128, 256 in all within a row
- tgt_lengths: int32 [32, 8], P(('dp', 'fsdp')), may hold values from 1 to 128, 256 in all within a row
- enc_attn_in: bfloat16 [512, 1536], P('fsdp'), may hold values from -0.25 to 0.25
- enc_attn_out: bfloat16 [512, 512], P('fsdp'), may hold values from -0.75 to 0.75
- enc_ffn_in: bfloat16 [512, 2048], P('fsdp'), may hold values from -0.25 to 0.25
- enc_ffn_out: bfloat16 [2048, 512], P('fsdp'), may hold values from -0.125 to 0.125
- enc_gain: bfloat16 [2, 512], P(None, 'fsdp'), may hold values from 0.5 to 1.5
- enc_bias: bfloat16 [2, 512], P(None, 'fsdp'), may hold values from -3 to 3
- dec_self_in: bfloat16 [512, 1536], P('fsdp'), may hold values from -0.25 to 0.25
- dec_self_out: bfloat16 [512, 512], P('fsdp'), may hold values from -0.75 to 0.75
- dec_cross_q: bfloat16 [512, 512], P('fsdp'), may hold values from -0.25 to 0.25
- dec_cross_kv: bfloat16 [512, 1024], P('fsdp'), may hold values from -0.25 to 0.25
- dec_cross_out: bfloat16 [512, 512], P('fsdp'), may hold values from -0.75 to 0.75
- dec_ffn_in: bfloat16 [512, 2048], P('fsdp'), may hold values from -0.25 to 0.25
- dec_ffn_out: bfloat16 [2048, 512], P('fsdp'), may hold values from -0.125 to 0.125
- dec_gain: bfloat16 [3, 512], P(None, 'fsdp'), may hold values from 0.5 to 1.5
- dec_bias: bfloat16 [3, 512], P(None, 'fsdp'), may hold values from -3 to 3
Outputs:
- first_out: bfloat16 [8192, 512], P(('dp', 'fsdp'))
- second_out: bfloat16 [8192, 512], P(('dp', 'fsdp'))
- source_grad: float32 [8192, 512], P(('dp', 'fsdp'))
- first_grad: float32 [8192, 512], P(('dp', 'fsdp'))
- enc_attn_in_grad: float32 [512, 1536], P('fsdp')
- enc_attn_out_grad: float32 [512, 512], P('fsdp')
- enc_ffn_in_grad: float32 [512, 2048], P('fsdp')
- enc_ffn_out_grad: float32 [2048, 512], P('fsdp')
- enc_gain_grad: float32 [2, 512], P(None, 'fsdp')
- enc_bias_grad: float32 [2, 512], P(None, 'fsdp')
- dec_self_in_grad: float32 [512, 1536], P('fsdp')
- dec_self_out_grad: float32 [512, 512], P('fsdp')
- dec_cross_q_grad: float32 [512, 512], P('fsdp')
- dec_cross_kv_grad: float32 [512, 1024], P('fsdp')
- dec_cross_out_grad: float32 [512, 512], P('fsdp')
- dec_ffn_in_grad: float32 [512, 2048], P('fsdp')
- dec_ffn_out_grad: float32 [2048, 512], P('fsdp')
- dec_gain_grad: float32 [3, 512], P(None, 'fsdp')
- dec_bias_grad: float32 [3, 512], P(None, 'fsdp')
Inputs may be any that keep to these rules, and one draw needn't show every extreme that they name: `src_lengths`: row r lists in order the lengths of the 8 source sentences that fill tokens r * 256 to (r + 1) * 256 - 1 of source; they sum to 256; sentence k of a row pairs with sentence k of the same row of tgt_lengths. `tgt_lengths`: row r lists in order the lengths of the 8 target sentences that fill tokens r * 256 to (r + 1) * 256 - 1 of first_in, second_in and the cotangents; they sum to 256.
All inputs are finite; a program needn't handle non-finite values.
Results may differ from a plain program's by a relative error of at most 0.029.
Values may be sent and summed in bfloat16 or wider, within the bound.
No kernel may reach another device: no remote copies, remote signals or barrier semaphores. Data moves between devices by JAX's collectives and lax.ppermute only.
A program may use at most 192 MiB of HBM per device.

v0:
```python
import jax
import jax.numpy as jnp
from jax import lax
from jax.sharding import PartitionSpec as P

D = 512
HEADS = 8


EPSILON = 1e-05
MASKED = -1000000000.0


def layer_norm(values, norm_gain, norm_bias):
    centre = values - jnp.mean(values, axis=-1, keepdims=True)
    spread = jnp.mean(centre * centre, axis=-1, keepdims=True)
    return centre * lax.rsqrt(spread + EPSILON) * norm_gain + norm_bias


def gelu_tanh(values):
    return jax.nn.gelu(values, approximate=True)


def norm_back(values, norm_gain, norm_bias, grad_normed):
    unused, pullback = jax.vjp(layer_norm, values, norm_gain, norm_bias)
    return pullback(grad_normed)


def project(left, right):
    return jnp.dot(left, right, preferred_element_type=jnp.float32)


def contract_rows(left, right):
    return lax.dot_general(
        left, right, (((0,), (0,)), ((), ())), preferred_element_type=jnp.float32
    )


def times_transposed(left, right):
    return lax.dot_general(
        left, right, (((1,), (1,)), ((), ())), preferred_element_type=jnp.float32
    )


def add_trees(first_tree, second_tree):
    return jax.tree.map(jnp.add, first_tree, second_tree)


def segments(lengths, count):
    sent_ends = jnp.cumsum(lengths[0], dtype=jnp.int32)
    places = jnp.arange(count, dtype=jnp.int32)
    return jnp.sum(
        (places[:, None] >= sent_ends[None, :]).astype(jnp.int32), axis=1, dtype=jnp.int32
    )


def split_heads(matrix):
    return matrix.reshape(matrix.shape[0], HEADS, matrix.shape[1] // HEADS)


def head_scores(queries, key_rows, allowed):
    scaling = (queries.shape[1] // HEADS) ** (-0.5)
    scores = (
        jnp.einsum(
            "qhd,khd->hqk",
            split_heads(queries),
            split_heads(key_rows),
            preferred_element_type=jnp.float32,
        )
        * scaling
    )
    return jnp.where(allowed[None], scores, MASKED)


def attend(queries, key_rows, value_rows, allowed):
    scores = head_scores(queries, key_rows, allowed)
    log_total = jax.nn.logsumexp(scores, axis=-1, keepdims=True)
    attn_probs = jnp.exp(scores - log_total).astype(jnp.bfloat16)
    mixed_heads = jnp.einsum(
        "hqk,khd->qhd", attn_probs, split_heads(value_rows), preferred_element_type=jnp.float32
    )
    return (mixed_heads.reshape(queries.shape).astype(jnp.bfloat16), log_total)


def attend_back(queries, key_rows, value_rows, allowed, log_total, grad_mixed):
    scaling = (queries.shape[1] // HEADS) ** (-0.5)
    attn_probs = jnp.exp(head_scores(queries, key_rows, allowed) - log_total)
    grad_heads = split_heads(grad_mixed)
    grad_values = jnp.einsum(
        "hqk,qhd->khd",
        attn_probs.astype(jnp.bfloat16),
        grad_heads,
        preferred_element_type=jnp.float32,
    )
    grad_probs = jnp.einsum(
        "qhd,khd->hqk", grad_heads, split_heads(value_rows), preferred_element_type=jnp.float32
    )
    grad_scores = attn_probs * (
        grad_probs - jnp.sum(attn_probs * grad_probs, axis=-1, keepdims=True)
    )
    grad_low = grad_scores.astype(jnp.bfloat16)
    grad_queries = (
        jnp.einsum(
            "hqk,khd->qhd", grad_low, split_heads(key_rows), preferred_element_type=jnp.float32
        )
        * scaling
    )
    grad_keys = (
        jnp.einsum(
            "hqk,qhd->khd", grad_low, split_heads(queries), preferred_element_type=jnp.float32
        )
        * scaling
    )
    return (
        grad_queries.reshape(queries.shape).astype(jnp.bfloat16),
        grad_keys.reshape(key_rows.shape).astype(jnp.bfloat16),
        grad_values.reshape(value_rows.shape).astype(jnp.bfloat16),
    )


def self_forward(inputs, norm_gain, norm_bias, w_joined, w_out, allowed):
    normed = layer_norm(inputs, norm_gain, norm_bias).astype(jnp.bfloat16)
    joined = project(normed, w_joined).astype(jnp.bfloat16)
    queries, key_rows, value_rows = (joined[:, :D], joined[:, D : 2 * D], joined[:, 2 * D :])
    mixed_heads, log_total = attend(queries, key_rows, value_rows, allowed)
    return (
        inputs + project(mixed_heads, w_out),
        (normed, queries, key_rows, value_rows, mixed_heads, log_total),
    )


def self_back(inputs, kept, grad_out, norm_gain, norm_bias, w_joined, w_out, allowed):
    normed, queries, key_rows, value_rows, mixed_heads, log_total = kept
    grad_branch = grad_out.astype(jnp.bfloat16)
    grad_w_out = contract_rows(mixed_heads, grad_branch)
    grad_mixed = times_transposed(grad_branch, w_out).astype(jnp.bfloat16)
    grad_query, grad_key, grad_value = attend_back(
        queries, key_rows, value_rows, allowed, log_total, grad_mixed
    )
    grad_joined = jnp.concatenate((grad_query, grad_key, grad_value), axis=1)
    grad_w_joined = contract_rows(normed, grad_joined)
    grad_normed = times_transposed(grad_joined, w_joined)
    grad_inputs, grad_gain, grad_bias = norm_back(inputs, norm_gain, norm_bias, grad_normed)
    return (grad_out + grad_inputs, (grad_w_joined, grad_w_out), grad_gain, grad_bias)


def cross_forward(inputs, norm_gain, norm_bias, w_query, w_pair, w_out, memory, allowed):
    normed = layer_norm(inputs, norm_gain, norm_bias).astype(jnp.bfloat16)
    queries = project(normed, w_query).astype(jnp.bfloat16)
    paired = project(memory, w_pair).astype(jnp.bfloat16)
    key_rows, value_rows = (paired[:, :D], paired[:, D:])
    mixed_heads, log_total = attend(queries, key_rows, value_rows, allowed)
    return (
        inputs + project(mixed_heads, w_out),
        (normed, queries, key_rows, value_rows, mixed_heads, log_total),
    )


def cross_back(
    inputs, kept, grad_out, norm_gain, norm_bias, w_query, w_pair, w_out, memory, allowed
):
    normed, queries, key_rows, value_rows, mixed_heads, log_total = kept
    grad_branch = grad_out.astype(jnp.bfloat16)
    grad_w_out = contract_rows(mixed_heads, grad_branch)
    grad_mixed = times_transposed(grad_branch, w_out).astype(jnp.bfloat16)
    grad_query, grad_key, grad_value = attend_back(
        queries, key_rows, value_rows, allowed, log_total, grad_mixed
    )
    grad_pair = jnp.concatenate((grad_key, grad_value), axis=1)
    grad_w_pair = contract_rows(memory, grad_pair)
    grad_memory = times_transposed(grad_pair, w_pair)
    grad_w_query = contract_rows(normed, grad_query)
    grad_normed = times_transposed(grad_query, w_query)
    grad_inputs, grad_gain, grad_bias = norm_back(inputs, norm_gain, norm_bias, grad_normed)
    return (
        grad_out + grad_inputs,
        grad_memory,
        (grad_w_query, grad_w_pair, grad_w_out),
        grad_gain,
        grad_bias,
    )


def ffn_forward(inputs, norm_gain, norm_bias, w_in, w_out):
    normed = layer_norm(inputs, norm_gain, norm_bias).astype(jnp.bfloat16)
    up_proj = project(normed, w_in)
    activated = gelu_tanh(up_proj).astype(jnp.bfloat16)
    return (inputs + project(activated, w_out), (normed, up_proj, activated))


def ffn_back(inputs, kept, grad_out, norm_gain, norm_bias, w_in, w_out):
    normed, up_proj, activated = kept
    grad_branch = grad_out.astype(jnp.bfloat16)
    grad_w_out = contract_rows(activated, grad_branch)
    grad_active = times_transposed(grad_branch, w_out)
    unused, pullback = jax.vjp(gelu_tanh, up_proj)
    grad_up = pullback(grad_active)[0].astype(jnp.bfloat16)
    grad_w_in = contract_rows(normed, grad_up)
    grad_normed = times_transposed(grad_up, w_in)
    grad_inputs, grad_gain, grad_bias = norm_back(inputs, norm_gain, norm_bias, grad_normed)
    return (grad_out + grad_inputs, (grad_w_in, grad_w_out), grad_gain, grad_bias)


def encoder_forward(source_rows, weights, source_mask):
    w_joined, w_out, w_ffn_in, w_ffn_out, norm_gains, norm_biases = weights
    gain_rows = norm_gains.astype(jnp.float32)
    bias_rows = norm_biases.astype(jnp.float32)
    hidden, kept_self = self_forward(
        source_rows, gain_rows[0], bias_rows[0], w_joined, w_out, source_mask
    )
    outputs, kept_ffn = ffn_forward(hidden, gain_rows[1], bias_rows[1], w_ffn_in, w_ffn_out)
    return (outputs, (hidden, kept_self, kept_ffn))


def encoder_back(source_rows, kept, grad_out, weights, source_mask):
    hidden, kept_self, kept_ffn = kept
    w_joined, w_out, w_ffn_in, w_ffn_out, norm_gains, norm_biases = weights
    gain_rows = norm_gains.astype(jnp.float32)
    bias_rows = norm_biases.astype(jnp.float32)
    grad_hidden, ffn_grads, gain_ffn, bias_ffn = ffn_back(
        hidden, kept_ffn, grad_out, gain_rows[1], bias_rows[1], w_ffn_in, w_ffn_out
    )
    grad_source, self_grads, gain_self, bias_self = self_back(
        source_rows,
        kept_self,
        grad_hidden,
        gain_rows[0],
        bias_rows[0],
        w_joined,
        w_out,
        source_mask,
    )
    return (
        grad_source,
        (
            self_grads[0],
            self_grads[1],
            ffn_grads[0],
            ffn_grads[1],
            jnp.stack((gain_self, gain_ffn)),
            jnp.stack((bias_self, bias_ffn)),
        ),
    )


def decoder_forward(inputs, memory, weights, target_mask, cross_mask):
    (
        w_joined,
        w_self_out,
        w_query,
        w_pair,
        w_cross_out,
        w_ffn_in,
        w_ffn_out,
        norm_gains,
        norm_biases,
    ) = weights
    gain_rows = norm_gains.astype(jnp.float32)
    bias_rows = norm_biases.astype(jnp.float32)
    hidden_one, kept_self = self_forward(
        inputs, gain_rows[0], bias_rows[0], w_joined, w_self_out, target_mask
    )
    hidden_two, kept_cross = cross_forward(
        hidden_one, gain_rows[1], bias_rows[1], w_query, w_pair, w_cross_out, memory, cross_mask
    )
    outputs, kept_ffn = ffn_forward(hidden_two, gain_rows[2], bias_rows[2], w_ffn_in, w_ffn_out)
    return (outputs, (hidden_one, hidden_two, kept_self, kept_cross, kept_ffn))


def decoder_back(inputs, kept, grad_out, memory, weights, target_mask, cross_mask):
    hidden_one, hidden_two, kept_self, kept_cross, kept_ffn = kept
    (
        w_joined,
        w_self_out,
        w_query,
        w_pair,
        w_cross_out,
        w_ffn_in,
        w_ffn_out,
        norm_gains,
        norm_biases,
    ) = weights
    gain_rows = norm_gains.astype(jnp.float32)
    bias_rows = norm_biases.astype(jnp.float32)
    grad_two, ffn_grads, gain_ffn, bias_ffn = ffn_back(
        hidden_two, kept_ffn, grad_out, gain_rows[2], bias_rows[2], w_ffn_in, w_ffn_out
    )
    grad_one, grad_memory, cross_grads, gain_cross, bias_cross = cross_back(
        hidden_one,
        kept_cross,
        grad_two,
        gain_rows[1],
        bias_rows[1],
        w_query,
        w_pair,
        w_cross_out,
        memory,
        cross_mask,
    )
    grad_inputs, self_grads, gain_self, bias_self = self_back(
        inputs, kept_self, grad_one, gain_rows[0], bias_rows[0], w_joined, w_self_out, target_mask
    )
    grads = (
        self_grads[0],
        self_grads[1],
        cross_grads[0],
        cross_grads[1],
        cross_grads[2],
        ffn_grads[0],
        ffn_grads[1],
        jnp.stack((gain_self, gain_cross, gain_ffn)),
        jnp.stack((bias_self, bias_cross, bias_ffn)),
    )
    return (grad_inputs, grad_memory, grads)


def body(
    source,
    first_in,
    second_in,
    cot_first,
    cot_second,
    src_lengths,
    tgt_lengths,
    enc_attn_in,
    enc_attn_out,
    enc_ffn_in,
    enc_ffn_out,
    enc_gain,
    enc_bias,
    dec_self_in,
    dec_self_out,
    dec_cross_q,
    dec_cross_kv,
    dec_cross_out,
    dec_ffn_in,
    dec_ffn_out,
    dec_gain,
    dec_bias,
):
    token_count = source.shape[0]
    source_ids = segments(src_lengths, token_count)
    target_ids = segments(tgt_lengths, token_count)
    source_mask = source_ids[:, None] == source_ids[None, :]
    target_mask = target_ids[:, None] == target_ids[None, :]
    cross_mask = target_ids[:, None] == source_ids[None, :]
    enc_weights = (
        lax.all_gather(enc_attn_in, "fsdp", axis=0, tiled=True),
        lax.all_gather(enc_attn_out, "fsdp", axis=0, tiled=True),
        lax.all_gather(enc_ffn_in, "fsdp", axis=0, tiled=True),
        lax.all_gather(enc_ffn_out, "fsdp", axis=0, tiled=True),
        lax.all_gather(enc_gain, "fsdp", axis=1, tiled=True),
        lax.all_gather(enc_bias, "fsdp", axis=1, tiled=True),
    )
    source_rows = source.astype(jnp.float32)
    encoded, enc_kept = encoder_forward(source_rows, enc_weights, source_mask)
    memory = encoded.astype(jnp.bfloat16)
    pass_inputs = (first_in.astype(jnp.float32), second_in.astype(jnp.float32))
    pass_weights = []
    pass_kept = []
    pass_outputs = []
    for pass_index in range(2):
        gathered = (
            lax.all_gather(dec_self_in, "fsdp", axis=0, tiled=True),
            lax.all_gather(dec_self_out, "fsdp", axis=0, tiled=True),
            lax.all_gather(dec_cross_q, "fsdp", axis=0, tiled=True),
            lax.all_gather(dec_cross_kv, "fsdp", axis=0, tiled=True),
            lax.all_gather(dec_cross_out, "fsdp", axis=0, tiled=True),
            lax.all_gather(dec_ffn_in, "fsdp", axis=0, tiled=True),
            lax.all_gather(dec_ffn_out, "fsdp", axis=0, tiled=True),
            lax.all_gather(dec_gain, "fsdp", axis=1, tiled=True),
            lax.all_gather(dec_bias, "fsdp", axis=1, tiled=True),
        )
        outputs, kept = decoder_forward(
            pass_inputs[pass_index], memory, gathered, target_mask, cross_mask
        )
        pass_weights.append(gathered)
        pass_kept.append(kept)
        pass_outputs.append(outputs.astype(jnp.bfloat16))
    cotangents = (cot_first.astype(jnp.float32), cot_second.astype(jnp.float32))
    grad_memory = jnp.zeros(encoded.shape, jnp.float32)
    input_grads = [None, None]
    dec_parts = []
    for pass_index in (1, 0):
        grad_inputs, grad_part, grads = decoder_back(
            pass_inputs[pass_index],
            pass_kept[pass_index],
            cotangents[pass_index],
            memory,
            pass_weights[pass_index],
            target_mask,
            cross_mask,
        )
        grad_memory = grad_memory + grad_part
        input_grads[pass_index] = grad_inputs
        dec_parts.append(
            (
                lax.psum_scatter(grads[0], "fsdp", scatter_dimension=0, tiled=True),
                lax.psum_scatter(grads[1], "fsdp", scatter_dimension=0, tiled=True),
                lax.psum_scatter(grads[2], "fsdp", scatter_dimension=0, tiled=True),
                lax.psum_scatter(grads[3], "fsdp", scatter_dimension=0, tiled=True),
                lax.psum_scatter(grads[4], "fsdp", scatter_dimension=0, tiled=True),
                lax.psum_scatter(grads[5], "fsdp", scatter_dimension=0, tiled=True),
                lax.psum_scatter(grads[6], "fsdp", scatter_dimension=0, tiled=True),
                lax.psum_scatter(grads[7], "fsdp", scatter_dimension=1, tiled=True),
                lax.psum_scatter(grads[8], "fsdp", scatter_dimension=1, tiled=True),
            )
        )
    dec_sum = add_trees(dec_parts[0], dec_parts[1])
    grad_source, enc_grads = encoder_back(
        source_rows, enc_kept, grad_memory, enc_weights, source_mask
    )
    enc_shards = (
        lax.psum_scatter(enc_grads[0], "fsdp", scatter_dimension=0, tiled=True),
        lax.psum_scatter(enc_grads[1], "fsdp", scatter_dimension=0, tiled=True),
        lax.psum_scatter(enc_grads[2], "fsdp", scatter_dimension=0, tiled=True),
        lax.psum_scatter(enc_grads[3], "fsdp", scatter_dimension=0, tiled=True),
        lax.psum_scatter(enc_grads[4], "fsdp", scatter_dimension=1, tiled=True),
        lax.psum_scatter(enc_grads[5], "fsdp", scatter_dimension=1, tiled=True),
    )
    summed = (
        lax.psum(enc_shards[0].astype(jnp.bfloat16), "dp").astype(jnp.float32),
        lax.psum(enc_shards[1].astype(jnp.bfloat16), "dp").astype(jnp.float32),
        lax.psum(enc_shards[2].astype(jnp.bfloat16), "dp").astype(jnp.float32),
        lax.psum(enc_shards[3].astype(jnp.bfloat16), "dp").astype(jnp.float32),
        lax.psum(enc_shards[4].astype(jnp.bfloat16), "dp").astype(jnp.float32),
        lax.psum(enc_shards[5].astype(jnp.bfloat16), "dp").astype(jnp.float32),
        lax.psum(dec_sum[0].astype(jnp.bfloat16), "dp").astype(jnp.float32),
        lax.psum(dec_sum[1].astype(jnp.bfloat16), "dp").astype(jnp.float32),
        lax.psum(dec_sum[2].astype(jnp.bfloat16), "dp").astype(jnp.float32),
        lax.psum(dec_sum[3].astype(jnp.bfloat16), "dp").astype(jnp.float32),
        lax.psum(dec_sum[4].astype(jnp.bfloat16), "dp").astype(jnp.float32),
        lax.psum(dec_sum[5].astype(jnp.bfloat16), "dp").astype(jnp.float32),
        lax.psum(dec_sum[6].astype(jnp.bfloat16), "dp").astype(jnp.float32),
        lax.psum(dec_sum[7].astype(jnp.bfloat16), "dp").astype(jnp.float32),
        lax.psum(dec_sum[8].astype(jnp.bfloat16), "dp").astype(jnp.float32),
    )
    return (
        pass_outputs[0],
        pass_outputs[1],
        grad_source,
        input_grads[0],
        summed[0],
        summed[1],
        summed[2],
        summed[3],
        summed[4],
        summed[5],
        summed[6],
        summed[7],
        summed[8],
        summed[9],
        summed[10],
        summed[11],
        summed[12],
        summed[13],
        summed[14],
    )


def solution(mesh):
    placed = (
        P(("dp", "fsdp"), None),
        P(("dp", "fsdp"), None),
        P(("dp", "fsdp"), None),
        P(("dp", "fsdp"), None),
        P(("dp", "fsdp"), None),
        P(("dp", "fsdp"), None),
        P(("dp", "fsdp"), None),
        P("fsdp", None),
        P("fsdp", None),
        P("fsdp", None),
        P("fsdp", None),
        P(None, "fsdp"),
        P(None, "fsdp"),
        P("fsdp", None),
        P("fsdp", None),
        P("fsdp", None),
        P("fsdp", None),
        P("fsdp", None),
        P("fsdp", None),
        P("fsdp", None),
        P(None, "fsdp"),
        P(None, "fsdp"),
    )
    return jax.shard_map(
        body,
        mesh=mesh,
        in_specs=placed,
        out_specs=(
            P(("dp", "fsdp"), None),
            P(("dp", "fsdp"), None),
            P(("dp", "fsdp"), None),
            P(("dp", "fsdp"), None),
            P("fsdp", None),
            P("fsdp", None),
            P("fsdp", None),
            P("fsdp", None),
            P(None, "fsdp"),
            P(None, "fsdp"),
            P("fsdp", None),
            P("fsdp", None),
            P("fsdp", None),
            P("fsdp", None),
            P("fsdp", None),
            P("fsdp", None),
            P("fsdp", None),
            P(None, "fsdp"),
            P(None, "fsdp"),
        ),
        check_vma=False,
    )
```

profile of v0, /device:TPU:0, one launch (start us, length us, event | category | flops | bytes accessed | tf_op | source)
XLA Modules:
  0.0 1444.1 jit_solution(12591527146616710766)
XLA Ops:
  12.0 23.4 %all-gather.1 = bf16[16,32,3]{1,2,0:T(4,128)(2,1)S(1)} all-gather(bf16[1,32,3]{1,2,0:T(4,128)(2,1)} %bitcast.410), channel_id=1, replica_groups=mesh['dp'=2,'fsdp'=16] {'fsdp'}, dimensions={0}, use_global_device_ids=true | all-gather | bytes 3264 | tf_op jit(solution)/shard_map/all_gather | solution.py:372
  36.1 17.7 %all-gather = bf16[16,32,3]{1,2,0:T(4,128)(2,1)S(1)} all-gather(bf16[1,32,3]{1,2,0:T(4,128)(2,1)} %bitcast.411), channel_id=1, replica_groups=mesh['dp'=2,'fsdp'=16] {'fsdp'}, dimensions={0}, use_global_device_ids=true | all-gather | bytes 3264 | tf_op jit(solution)/shard_map/all_gather | solution.py:371
  58.4 22.3 %all_gather.57 = bf16[512,512]{1,0:T(8,128)(2,1)} all-gather(bf16[32,512]{1,0:T(8,128)(2,1)} %param.36), channel_id=1, replica_groups=mesh['dp'=2,'fsdp'=16] {'fsdp'}, dimensions={0}, use_global_device_ids=true | all-gather | bytes 557056 | tf_op jit(solution)/shard_map/all_gather | solution.py:365
  80.7 17.4 %all-gather.3 = bf16[16,32,2]{1,2,0:T(2,128)(2,1)S(1)} all-gather(bf16[1,32,2]{1,2,0:T(2,128)(2,1)S(1)} %bitcast.412), channel_id=1, replica_groups=mesh['dp'=2,'fsdp'=16] {'fsdp'}, dimensions={0}, use_global_device_ids=true | all-gather | bytes 2176 | tf_op jit(solution)/shard_map/all_gather | solution.py:353
  98.8 18.5 %all-gather.2 = bf16[16,32,2]{1,2,0:T(2,128)(2,1)S(1)} all-gather(bf16[1,32,2]{1,2,0:T(2,128)(2,1)S(1)} %bitcast.413), channel_id=1, replica_groups=mesh['dp'=2,'fsdp'=16] {'fsdp'}, dimensions={0}, use_global_device_ids=true | all-gather | bytes 2176 | tf_op jit(solution)/shard_map/all_gather | solution.py:352
  119.0 21.5 %all_gather.61 = bf16[512,512]{1,0:T(8,128)(2,1)} all-gather(bf16[32,512]{1,0:T(8,128)(2,1)S(1)} %copy-done.173), channel_id=1, replica_groups=mesh['dp'=2,'fsdp'=16] {'fsdp'}, dimensions={0}, use_global_device_ids=true | all-gather | bytes 557056 | tf_op jit(solution)/shard_map/all_gather | solution.py:349
  140.4 20.4 %all_gather.65 = bf16[512,512]{1,0:T(8,128)(2,1)S(1)} all-gather(bf16[32,512]{1,0:T(8,128)(2,1)S(1)} %copy-done.174), channel_id=1, replica_groups=mesh['dp'=2,'fsdp'=16] {'fsdp'}, dimensions={0}, use_global_device_ids=true | all-gather | bytes 557056 | tf_op jit(solution)/shard_map/all_gather | solution.py:366
  160.9 22.5 %all_gather.66 = bf16[512,512]{1,0:T(8,128)(2,1)} all-gather(bf16[32,512]{1,0:T(8,128)(2,1)S(1)} %copy-done.175), channel_id=1, replica_groups=mesh['dp'=2,'fsdp'=16] {'fsdp'}, dimensions={0}, use_global_device_ids=true | all-gather | bytes 557056 | tf_op jit(solution)/shard_map/all_gather | solution.py:368
  185.3 2.0 convolution_convert_fusion.2
  190.4 2.1 convolution_convert_fusion.1
  194.5 1.9 copy.236
  206.7 1.8 copy.240
  208.6 2.2 convolution_convert_fusion
  212.9 1.9 copy.245
  219.8 1.8 copy.247
  221.6 3.9 fusion.125
  225.5 3.8 fusion.26
  238.7 2.2 convolution_convert_fusion.17
  245.5 19.9 %all-gather.24.cloned.1.call-done = bf16[2048,512]{1,0:T(8,128)(2,1)} async-done(((bf16[128,512]{1,0:T(8,128)(2,1)}), bf16[2048,512]{1,0:T(8,128)(2,1)}) %all-gather.24.cloned.1.call-update) | async-done | bytes 2097168 | tf_op jit(solution)/shard_map/all_gather | solution.py:370
  265.4 3.9 fusion.159
  269.2 2.1 fusion.157
  271.3 36.4 %all-gather.22.cloned.1.call-done = bf16[512,2048]{1,0:T(8,128)(2,1)} async-done(((bf16[32,2048]{1,0:T(8,128)(2,1)}), bf16[512,2048]{1,0:T(8,128)(2,1)}) %all-gather.22.cloned.1.call-update) | async-done | bytes 2097168 | tf_op jit(solution)/shard_map/all_gather | solution.py:369
  307.7 5.6 fusion.20
  315.5 3.2 fusion.13
  324.2 1.8 copy.249
  326.0 3.0 convolution_convert_fusion.12
  329.0 2.0 multiply_reduce_fusion.4
  332.9 1.8 copy.252
  334.7 2.3 convolution_convert_fusion.10
  344.6 1.8 fusion.6
  350.2 1.8 copy.255
  352.0 3.0 convolution_convert_fusion.8
  364.2 1.8 copy.260
  366.0 2.2 convolution_convert_fusion.6
  375.7 2.2 convolution_convert_fusion.4
  387.8 2.8 fusion.132
  402.5 1.9 convolution_add_fusion.3
  405.5 2.4 fusion.76
  409.8 2.5 convolution_add_fusion
  413.7 2.9 fusion.124
  417.6 4.6 fusion.93
  423.2 2.1 fusion.128
  425.3 3.0 convolution_add_fusion.2
  429.3 2.7 fusion.130
  432.0 3.2 convolution_add_fusion.1
  437.2 3.3 reduce-scatter.46.cloned.1.call-done
  441.8 56.6 %reduce-scatter.48.cloned.1.call-done = f32[32,2]{1,0:T(8,128)} async-done(((f32[512,2]{1,0:T(8,128)}), f32[32,2]{1,0:T(8,128)}) %reduce-scatter.48.cloned.1.call-update) | async-done | bytes 272
  499.7 56.4 %reduce-scatter.50.cloned.1.call-done = f32[32,3]{1,0:T(8,128)} async-done(((f32[512,3]{1,0:T(8,128)}), f32[32,3]{1,0:T(8,128)}) %reduce-scatter.50.cloned.1.call-update) | async-done | bytes 400
  557.5 56.5 %reduce-scatter.52.cloned.1.call-done = f32[32,3]{1,0:T(8,128)} async-done(((f32[512,3]{1,0:T(8,128)}), f32[32,3]{1,0:T(8,128)}) %reduce-scatter.52.cloned.1.call-update) | async-done | bytes 400
  615.4 58.6 %reduce-scatter.26.cloned.1.call-done = f32[32,512]{1,0:T(8,128)} async-done(((f32[512,512]{1,0:T(8,128)}), f32[32,512]{1,0:T(8,128)}) %reduce-scatter.26.cloned.1.call-update) | async-done | bytes 65552 | tf_op jit(solution)/shard_map/reduce_scatter | solution.py:415
  675.5 59.0 %reduce-scatter.34.cloned.1.call-done = f32[32,512]{1,0:T(8,128)} async-done(((f32[512,512]{1,0:T(8,128)}), f32[32,512]{1,0:T(8,128)}) %reduce-scatter.34.cloned.1.call-update) | async-done | bytes 65552 | tf_op jit(solution)/shard_map/reduce_scatter | solution.py:399
  735.9 58.4 %reduce-scatter.36.cloned.1.call-done = f32[32,512]{1,0:T(8,128)} async-done(((f32[512,512]{1,0:T(8,128)}), f32[32,512]{1,0:T(8,128)}) %reduce-scatter.36.cloned.1.call-update) | async-done | bytes 65552 | tf_op jit(solution)/shard_map/reduce_scatter | solution.py:400
  795.8 58.9 %reduce-scatter.40.cloned.1.call-done = f32[32,512]{1,0:T(8,128)} async-done(((f32[512,512]{1,0:T(8,128)}), f32[32,512]{1,0:T(8,128)}) %reduce-scatter.40.cloned.1.call-update) | async-done | bytes 65552 | tf_op jit(solution)/shard_map/reduce_scatter | solution.py:402
  856.2 2.4 add_add_fusion.7
  858.5 60.3 %reduce-scatter.38.cloned.1.call-done = f32[32,1024]{1,0:T(8,128)} async-done(((f32[512,1024]{1,0:T(8,128)}), f32[32,1024]{1,0:T(8,128)}) %reduce-scatter.38.cloned.1.call-update) | async-done | bytes 131088 | tf_op jit(solution)/shard_map/reduce_scatter | solution.py:401
  920.4 67.8 %reduce-scatter.24.cloned.1.call-done = f32[32,1536]{1,0:T(8,128)} async-done(((f32[512,1536]{1,0:T(8,128)}), f32[32,1536]{1,0:T(8,128)}) %reduce-scatter.24.cloned.1.call-update) | async-done | bytes 196624 | tf_op jit(solution)/shard_map/reduce_scatter | solution.py:414
  989.8 67.8 %reduce-scatter.32.cloned.1.call-done = f32[32,1536]{1,0:T(8,128)} async-done(((f32[512,1536]{1,0:T(8,128)}), f32[32,1536]{1,0:T(8,128)}) %reduce-scatter.32.cloned.1.call-update) | async-done | bytes 196624 | tf_op jit(solution)/shard_map/reduce_scatter | solution.py:398
  1059.2 74.1 %reduce-scatter.28.cloned.1.call-done = f32[32,2048]{1,0:T(8,128)} async-done(((f32[512,2048]{1,0:T(8,128)}), f32[32,2048]{1,0:T(8,128)}) %reduce-scatter.28.cloned.1.call-update) | async-done | bytes 262160 | tf_op jit(solution)/shard_map/reduce_scatter | solution.py:416
  1134.9 73.6 %reduce-scatter.30.cloned.1.call-done = f32[128,512]{1,0:T(8,128)} async-done(((f32[2048,512]{1,0:T(8,128)}), f32[128,512]{1,0:T(8,128)}) %reduce-scatter.30.cloned.1.call-update) | async-done | bytes 262160 | tf_op jit(solution)/shard_map/reduce_scatter | solution.py:417
  1210.2 74.1 %reduce-scatter.42.cloned.1.call-done = f32[32,2048]{1,0:T(8,128)} async-done(((f32[512,2048]{1,0:T(8,128)}), f32[32,2048]{1,0:T(8,128)}) %reduce-scatter.42.cloned.1.call-update) | async-done | bytes 262160 | tf_op jit(solution)/shard_map/reduce_scatter | solution.py:403
  1285.9 73.8 %reduce-scatter.44.cloned.1.call-done = f32[128,512]{1,0:T(8,128)} async-done(((f32[2048,512]{1,0:T(8,128)}), f32[128,512]{1,0:T(8,128)}) %reduce-scatter.44.cloned.1.call-update) | async-done | bytes 262160 | tf_op jit(solution)/shard_map/reduce_scatter | solution.py:404
  1361.4 3.3 fusion.27
  1366.3 19.6 %all-reduce.5.cloned.1.call-done = (bf16[32,512]{1,0:T(8,128)(2,1)}, bf16[2,32]{1,0:T(2,128)(2,1)}, bf16[2,32]{1,0:T(2,128)(2,1)}, bf16[32,512]{1,0:T(8,128)(2,1...) async-done(((bf16[32,512]{1,0:T(8,128)(2,1)}, bf16[2,32]{1,0:T(2,128)(2,1)}, bf16[2,32]{1,0:T(2,128)(2,1)}, ...) | async-done | bytes 131728 | tf_op jit(solution)/shard_map/psum | solution.py:423
  1396.2 29.7 %all-reduce.7.cloned.1.call-done = (bf16[32,1536]{1,0:T(8,128)(2,1)}, bf16[32,2048]{1,0:T(8,128)(2,1)}, bf16[128,512]{1,0:T(8,128)(2,1)}, bf16[32,1536]{1,0:T(8,...) async-done(((bf16[32,1536]{1,0:T(8,128)(2,1)}, bf16[32,2048]{1,0:T(8,128)(2,1)}, bf16[128,512]{1,0:T(8,128)(2,1)}, ...) | async-done | bytes 786448 | tf_op jit(solution)/shard_map/psum | solution.py:422
  (676 shorter events, 163.1 us)
Async XLA Ops:
  7.2 73.5 %copy-start.208 = (bf16[2,32]{1,0:T(2,128)(2,1)S(1)}, bf16[2,32]{1,0:T(2,128)(2,1)}, u32[]{:S(2)}) copy-start(bf16[2,32]{1,0:T(2,128)(2,1)} %param.34) | copy-start | bytes 388
  7.2 91.6 %copy-start.209 = (bf16[2,32]{1,0:T(2,128)(2,1)S(1)}, bf16[2,32]{1,0:T(2,128)(2,1)}, u32[]{:S(2)}) copy-start(bf16[2,32]{1,0:T(2,128)(2,1)} %param.33) | copy-start | bytes 388
  7.2 110.8 %copy-start.22 = (bf16[256,512]{1,0:T(8,128)(2,1)S(1)}, bf16[256,512]{1,0:T(8,128)(2,1)}, u32[]{:S(2)}) copy-start(bf16[256,512]{1,0:T(8,128)(2,1)} %param.22) | copy-start | bytes 786436
  7.2 111.7 %copy-start.173 = (bf16[32,512]{1,0:T(8,128)(2,1)S(1)}, bf16[32,512]{1,0:T(8,128)(2,1)}, u32[]{:S(2)}) copy-start(bf16[32,512]{1,0:T(8,128)(2,1)} %param.30) | copy-start | bytes 98308
  7.2 133.2 %copy-start.174 = (bf16[32,512]{1,0:T(8,128)(2,1)S(1)}, bf16[32,512]{1,0:T(8,128)(2,1)}, u32[]{:S(2)}) copy-start(bf16[32,512]{1,0:T(8,128)(2,1)} %param.37) | copy-start | bytes 98308
  7.2 153.7 %copy-start.175 = (bf16[32,512]{1,0:T(8,128)(2,1)S(1)}, bf16[32,512]{1,0:T(8,128)(2,1)}, u32[]{:S(2)}) copy-start(bf16[32,512]{1,0:T(8,128)(2,1)} %param.39) | copy-start | bytes 98308
  7.3 178.0 %all-gather.12.cloned.1.call-start = ((), (), s32[]{:S(2)}) async-start(), calls=%async_computation.15 | async-start | bytes 1671168 | tf_op jit(solution)/shard_map/all_gather | solution.py:364
  8.0 182.4 %all-gather.14.cloned.1.call-start = ((), (), s32[]{:S(2)}) async-start(), calls=%async_computation.16 | async-start | bytes 1671168 | tf_op jit(solution)/shard_map/all_gather | solution.py:348
  8.7 174.7 %copy-start.50 = (bf16[256,512]{1,0:T(8,128)(2,1)S(1)}, bf16[256,512]{1,0:T(8,128)(2,1)}, u32[]{:S(2)}) copy-start(bf16[256,512]{1,0:T(8,128)(2,1)} %param.24) | copy-start | bytes 786436
  8.7 212.8 %all-gather.16.cloned.1.call-start = ((), (), s32[]{:S(2)}) async-start(), calls=%async_computation.17 | async-start | bytes 2228224 | tf_op jit(solution)/shard_map/all_gather | solution.py:350
  9.5 216.1 %all-gather.18.cloned.1.call-start = ((), (), s32[]{:S(2)}) async-start(), calls=%async_computation.18 | async-start | bytes 2228224 | tf_op jit(solution)/shard_map/all_gather | solution.py:351
  10.1 219.3 %all-gather.20.cloned.1.call-start = ((), (), s32[]{:S(2)}) async-start(), calls=%async_computation.19 | async-start | bytes 1114112 | tf_op jit(solution)/shard_map/all_gather | solution.py:367
  10.6 254.7 %all-gather.24.cloned.1.call-start = ((), (), s32[]{:S(2)}) async-start(), calls=%async_computation.21 | async-start | bytes 2228224 | tf_op jit(solution)/shard_map/all_gather | solution.py:370
  11.2 296.5 %all-gather.22.cloned.1.call-start = ((), (), s32[]{:S(2)}) async-start(), calls=%async_computation.20 | async-start | bytes 2228224 | tf_op jit(solution)/shard_map/all_gather | solution.py:369
  12.0 428.5 %reduce-scatter.46.cloned.1.call-start = ((), (), s32[]{:S(2)}) async-start(), calls=%async_computation.33 | async-start | bytes 278528
  36.1 149.2 %copy-start.160 = (f32[1,512]{1,0:T(1,128)}, f32[1,512]{1,0:T(1,128)S(1)}, u32[]{:S(2)}) copy-start(f32[1,512]{1,0:T(1,128)S(1)} %get-tuple-element.85) | copy-start | bytes 6148
  53.9 131.4 %copy-start.30 = (bf16[256,512]{1,0:T(8,128)(2,1)S(1)}, bf16[256,512]{1,0:T(8,128)(2,1)}, u32[]{:S(2)}) copy-start(bf16[256,512]{1,0:T(8,128)(2,1)} %param.23) | copy-start | bytes 786436
  54.5 130.8 %copy-start.149 = (f32[1,512]{1,0:T(1,128)}, f32[1,512]{1,0:T(1,128)S(1)}, u32[]{:S(2)}) copy-start(f32[1,512]{1,0:T(1,128)S(1)} %get-tuple-element.82) | copy-start | bytes 6148
  55.6 129.7 %copy-start.181 = (f32[256]{0:T(256)}, f32[256]{0:T(256)S(1)}, u32[]{:S(2)}) copy-start(f32[256]{0:T(256)S(1)} %broadcast_multiply_fusion.7) | copy-start | bytes 3076
  56.7 24.0 %copy-start.190 = (f32[256]{0:T(256)}, f32[256]{0:T(256)S(1)}, u32[]{:S(2)}) copy-start(f32[256]{0:T(256)S(1)} %fusion.65) | copy-start | bytes 3076
  56.7 128.5 %copy-start.187 = (f32[256]{0:T(256)}, f32[256]{0:T(256)S(1)}, u32[]{:S(2)}) copy-start(f32[256]{0:T(256)S(1)} %fusion.99) | copy-start | bytes 3076
  98.8 91.6 %copy-start.163 = (f32[1,512]{1,0:T(1,128)}, f32[1,512]{1,0:T(1,128)S(1)}, u32[]{:S(2)}) copy-start(f32[1,512]{1,0:T(1,128)S(1)} %get-tuple-element.89) | copy-start | bytes 6148
  118.0 72.4 %copy-start.152 = (f32[1,512]{1,0:T(1,128)}, f32[1,512]{1,0:T(1,128)S(1)}, u32[]{:S(2)}) copy-start(f32[1,512]{1,0:T(1,128)S(1)} %get-tuple-element.87) | copy-start | bytes 6148
  118.1 69.2 %copy-start.167 = (f32[256]{0:T(256)}, f32[256]{0:T(256)S(1)}, u32[]{:S(2)}) copy-start(f32[256]{0:T(256)S(1)} %broadcast_multiply_fusion.6) | copy-start | bytes 3076
  118.4 65.1 %copy-start.192 = (f32[256]{0:T(256)}, f32[256]{0:T(256)S(1)}, u32[]{:S(2)}) copy-start(f32[256]{0:T(256)S(1)} %fusion.67) | copy-start | bytes 3076
  160.9 44.2 %copy-start.12 = (bf16[512,512]{1,0:T(8,128)(2,1)}, bf16[512,512]{1,0:T(8,128)(2,1)S(1)}, u32[]{:S(2)}) copy-start(bf16[512,512]{1,0:T(8,128)(2,1)S(1)} %all_gather.65) | copy-start | bytes 1572868
  187.5 15.6 %copy-start.73 = (bf16[256,512]{0,1:T(8,128)(2,1)}, bf16[256,512]{0,1:T(8,128)(2,1)S(1)}, u32[]{:S(2)}) copy-start(bf16[256,512]{0,1:T(8,128)(2,1)S(1)} %copy.229) | copy-start | bytes 786436
  194.5 5.6 copy-start.77
  211.7 5.0 copy-start.75
  217.6 4.0 copy-start.148
  217.6 4.0 copy-start.151
  217.6 4.0 copy-start.158
  217.6 4.0 copy-start.162
  218.5 7.0 copy-start.171
  218.7 6.8 copy-start.196
  218.7 6.8 copy-start.179
  241.4 78.9 %copy-start.185 = (f32[256]{0:T(256)}, f32[256]{0:T(256)S(1)}, u32[]{:S(2)}) copy-start(f32[256]{0:T(256)S(1)} %broadcast_multiply_fusion.3) | copy-start | bytes 3076
  265.3 3.9 copy-start.61
  269.2 38.5 %copy-start.154 = (f32[1,512]{1,0:T(1,128)S(1)}, f32[1,512]{1,0:T(1,128)}, u32[]{:S(2)}) copy-start(f32[1,512]{1,0:T(1,128)} %get-tuple-element.80) | copy-start | bytes 6148
  269.2 38.5 %copy-start.159 = (f32[1,512]{1,0:T(1,128)S(1)}, f32[1,512]{1,0:T(1,128)}, u32[]{:S(2)}) copy-start(f32[1,512]{1,0:T(1,128)} %get-tuple-element.83) | copy-start | bytes 6148
  307.7 5.7 copy-start.211
  313.4 5.3 copy-start.124
  337.1 5.8 copy-start.71
  370.9 4.8 copy-start.1
  386.3 112.1 %reduce-scatter.48.cloned.1.call-start = ((), (), s32[]{:S(2)}) async-start(), calls=%async_computation.34 | async-start | bytes 278528
  387.6 168.5 %reduce-scatter.50.cloned.1.call-start = ((), (), s32[]{:S(2)}) async-start(), calls=%async_computation.35 | async-start | bytes 278528
  387.8 5.5 copy-start.41
  387.8 5.5 copy-start.85
  390.6 4.0 copy-start.96
  391.5 222.5 %reduce-scatter.52.cloned.1.call-start = ((), (), s32[]{:S(2)}) async-start(), calls=%async_computation.36 | async-start | bytes 278528
  393.2 280.8 %reduce-scatter.26.cloned.1.call-start = ((), (), s32[]{:S(2)}) async-start(), calls=%async_computation.23 | async-start | bytes 1114112 | tf_op jit(solution)/shard_map/reduce_scatter | solution.py:415
  394.6 339.9 %reduce-scatter.34.cloned.1.call-start = ((), (), s32[]{:S(2)}) async-start(), calls=%async_computation.27 | async-start | bytes 1114112 | tf_op jit(solution)/shard_map/reduce_scatter | solution.py:399
  397.2 397.1 %reduce-scatter.36.cloned.1.call-start = ((), (), s32[]{:S(2)}) async-start(), calls=%async_computation.28 | async-start | bytes 1114112 | tf_op jit(solution)/shard_map/reduce_scatter | solution.py:400
  399.7 454.9 %reduce-scatter.40.cloned.1.call-start = ((), (), s32[]{:S(2)}) async-start(), calls=%async_computation.30 | async-start | bytes 1114112 | tf_op jit(solution)/shard_map/reduce_scatter | solution.py:402
  401.4 517.4 %reduce-scatter.38.cloned.1.call-start = ((), (), s32[]{:S(2)}) async-start(), calls=%async_computation.29 | async-start | bytes 2228224 | tf_op jit(solution)/shard_map/reduce_scatter | solution.py:401
  404.4 583.8 %reduce-scatter.24.cloned.1.call-start = ((), (), s32[]{:S(2)}) async-start(), calls=%async_computation.22 | async-start | bytes 3342336 | tf_op jit(solution)/shard_map/reduce_scatter | solution.py:414
  408.0 649.6 %reduce-scatter.32.cloned.1.call-start = ((), (), s32[]{:S(2)}) async-start(), calls=%async_computation.26 | async-start | bytes 3342336 | tf_op jit(solution)/shard_map/reduce_scatter | solution.py:398
  412.3 721.0 %reduce-scatter.28.cloned.1.call-start = ((), (), s32[]{:S(2)}) async-start(), calls=%async_computation.24 | async-start | bytes 4456448 | tf_op jit(solution)/shard_map/reduce_scatter | solution.py:416
  416.6 792.0 %reduce-scatter.30.cloned.1.call-start = ((), (), s32[]{:S(2)}) async-start(), calls=%async_computation.25 | async-start | bytes 4456448 | tf_op jit(solution)/shard_map/reduce_scatter | solution.py:417
  422.2 862.1 %reduce-scatter.42.cloned.1.call-start = ((), (), s32[]{:S(2)}) async-start(), calls=%async_computation.31 | async-start | bytes 4456448 | tf_op jit(solution)/shard_map/reduce_scatter | solution.py:403
  428.4 931.3 %reduce-scatter.44.cloned.1.call-start = ((), (), s32[]{:S(2)}) async-start(), calls=%async_computation.32 | async-start | bytes 4456448 | tf_op jit(solution)/shard_map/reduce_scatter | solution.py:404
  435.2 950.6 %all-reduce.5.cloned.1.call-start = ((), (), s32[]{:S(2)}) async-start(), calls=%async_computation.37 | async-start | bytes 268288 | tf_op jit(solution)/shard_map/psum | solution.py:423
  856.1 505.2 %copy-start.37 = (bf16[2048,512]{1,0:T(8,128)(2,1)S(1)}, bf16[2048,512]{1,0:T(8,128)(2,1)}, u32[]{:S(2)}) copy-start(bf16[2048,512]{1,0:T(8,128)(2,1)} %all-gather.24.cloned.1.call-done) | copy-start | bytes 6291460
  856.1 569.8 %all-reduce.7.cloned.1.call-start = ((), (), s32[]{:S(2)}) async-start(), calls=%async_computation.38 | async-start | bytes 1572864 | tf_op jit(solution)/shard_map/psum | solution.py:422
  (174 other events, 320.2 us)
Sparse Core Ops, SparseCore 0:
  10.4 42.4 all-gather.11
  55.1 39.3 all-gather.13
  96.6 41.9 all-gather.15
  140.6 42.5 all-gather.17
  185.2 37.6 all-gather.19
  225.0 40.3 all-gather.23
  267.5 40.1 all-gather.21
  386.5 54.0 reduce-scatter.45
  444.0 54.3 reduce-scatter.47
  501.8 54.3 reduce-scatter.49
  559.7 54.3 reduce-scatter.51
  617.5 56.4 reduce-scatter.25
  678.1 56.3 reduce-scatter.33
  737.9 56.3 reduce-scatter.35
  798.2 56.3 reduce-scatter.39
  858.2 60.5 reduce-scatter.37
  923.0 65.1 reduce-scatter.23
  992.4 65.1 reduce-scatter.31
  1061.9 71.3 reduce-scatter.27
  1137.0 71.5 reduce-scatter.29
  1212.9 71.3 reduce-scatter.41
  1288.2 71.5 reduce-scatter.43
  1364.3 21.4 all-reduce.4
  1390.3 35.5 all-reduce.6
where the time goes:
time: 1450 us; the launch traced here: 1440 us
  waiting for transfers between devices  1010 us (70%)
  blocking collectives  164 us (11%)
  matrix products  127 us (9%)
  local copies, waits for them, and re-layouts  67.1 us (5%)
  other arithmetic  59.1 us (4%)
  between operations  16.8 us (1%)
    unnamed x28, waiting for transfers between devices  177 us
    reduce_scatter x1, waiting for transfers between devices, body(): lax.psum_scatter(enc_grads[2], 'fsdp', scatter_dimension=0, tiled=True)  74.1 us
    reduce_scatter x1, waiting for transfers between devices, body(): lax.psum_scatter(grads[5], 'fsdp', scatter_dimension=0, tiled=True)  74.1 us
    reduce_scatter x1, waiting for transfers between devices, body(): lax.psum_scatter(grads[6], 'fsdp', scatter_dimension=0, tiled=True)  73.8 us
    reduce_scatter x1, waiting for transfers between devices, body(): lax.psum_scatter(enc_grads[3], 'fsdp', scatter_dimension=0, tiled=True)  73.6 us
    reduce_scatter x1, waiting for transfers between devices, body(): lax.psum_scatter(enc_grads[0], 'fsdp', scatter_dimension=0, tiled=True)  67.8 us
    reduce_scatter x1, waiting for transfers between devices, body(): lax.psum_scatter(grads[0], 'fsdp', scatter_dimension=0, tiled=True)  67.8 us
    reduce_scatter x1, waiting for transfers between devices, body(): lax.psum_scatter(grads[3], 'fsdp', scatter_dimension=0, tiled=True)  60.3 us
  transfers between devices with their start and end apart: 24, of which 19 were waited for; matrix products, arithmetic and copies ran while one was open for 10% of the time, Pallas kernels for 0%

commit v1 on v0

v1 whole, which is shorter than its diff:
```python
import functools

import jax
import jax.numpy as jnp
from jax import lax
from jax.experimental import pallas as pl
from jax.experimental.pallas import tpu as pltpu
from jax.sharding import PartitionSpec as P

D = 512
HEADS = 8
HEAD = 64
TOK = 256
FF = 2048
QUAD = 256
BLOCK = 32
EPSILON = 1e-05
MASKED = -1000000000.0
BF = jnp.bfloat16
F32 = jnp.float32
VMEM_LIMIT = 56 * 1024 * 1024


def dot(left, right):
    return lax.dot_general(left, right, (((1,), (0,)), ((), ())), preferred_element_type=F32)


def dot_nt(left, right):
    return lax.dot_general(left, right, (((1,), (1,)), ((), ())), preferred_element_type=F32)


def dot_tn(left, right):
    return lax.dot_general(left, right, (((0,), (0,)), ((), ())), preferred_element_type=F32)


def place_of(place, turn, first, second):
    which = place[3] ^ turn
    y = place[1] ^ jnp.where(which == 0, first, second)
    half = place[2] ^ jnp.where(which == 0, second, first)
    return y, half, which


def fetch(place, pieces, offset, held, sems):
    rows = held.shape[2] // 4
    copies = []
    for turn in range(2):
        for first in range(2):
            for second in range(2):
                y, half, which = place_of(place, turn, first, second)
                quarter = pl.multiple_of((2 * half + which) * rows, rows)
                for d in range(4):
                    copies.append(
                        pltpu.make_async_copy(
                            pieces[2 * turn + first].at[second, d, :, pl.ds(offset, rows)],
                            held.at[(place[0] + (4 - d)) & 3, pl.ds(2 * y, 2), pl.ds(quarter, rows)],
                            sems.at[len(copies)],
                        )
                    )
    for copy in copies:
        copy.start()
    return copies


def deliver(place, held, own, other, sems):
    rows = held.shape[2] // 4
    copies = []
    for turn in range(2):
        for first in range(2):
            for second in range(2):
                y, half, which = place_of(place, turn, first, second)
                quarter = pl.multiple_of((2 * half + which) * rows, rows)
                for d in range(4):
                    copies.append(
                        pltpu.make_async_copy(
                            held.at[(place[0] + d) & 3, pl.ds(2 * y, 2), pl.ds(quarter, rows)],
                            (own, other)[turn].at[first, second, d],
                            sems.at[len(copies)],
                        )
                    )
    for copy in copies:
        copy.start()
    return copies


def wait_all(copies):
    for copy in copies:
        copy.wait()


def column_block(held, index):
    return held[:, :, index * BLOCK : (index + 1) * BLOCK].reshape(D, D)


def row_block(held, index):
    return held[index, :, 4 * BLOCK : 8 * BLOCK].reshape(D, D)


def normed_of(values):
    centre = values - jnp.mean(values, axis=-1, keepdims=True)
    spread = jnp.mean(centre * centre, axis=-1, keepdims=True)
    inverse = lax.rsqrt(spread + EPSILON)
    return centre * inverse, inverse


def norm_back(unit, inverse, gain, grad_normed, norm_ref):
    norm_ref[0:1] = jnp.sum(grad_normed * unit, axis=0, keepdims=True)
    norm_ref[1:2] = jnp.sum(grad_normed, axis=0, keepdims=True)
    grad_unit = grad_normed * gain
    return (
        grad_unit
        - jnp.mean(grad_unit, axis=-1, keepdims=True)
        - unit * jnp.mean(grad_unit * unit, axis=-1, keepdims=True)
    ) * inverse


def mask_bias(key_lengths, query_lengths):
    key_place = lax.broadcasted_iota(jnp.int32, (TOK, 1), 0)
    query_place = lax.broadcasted_iota(jnp.int32, (1, TOK), 1)
    key_ids = jnp.zeros((TOK, 1), jnp.int32)
    query_ids = jnp.zeros((1, TOK), jnp.int32)
    key_end = jnp.int32(0)
    query_end = jnp.int32(0)
    for k in range(key_lengths.shape[1]):
        key_end = key_end + key_lengths[0, k]
        query_end = query_end + query_lengths[0, k]
        key_ids = key_ids + jnp.where(key_place >= key_end, 1, 0)
        query_ids = query_ids + jnp.where(query_place >= query_end, 1, 0)
    return jnp.where(key_ids == query_ids, 0.0, MASKED).astype(F32)


def lane_masks():
    head_of = lax.broadcasted_iota(jnp.int32, (1, QUAD), 1) // HEAD
    return [jnp.where(head_of == h, 1.0, 0.0).astype(BF) for h in range(QUAD // HEAD)]


def attend(queries, keys, values, bias, probs_ref, first):
    masks = lane_masks()
    outs = []
    for g in range(D // QUAD):
        cols = slice(g * QUAD, (g + 1) * QUAD)
        q, k, v = queries[:, cols], keys[:, cols], values[:, cols]
        total = None
        for h in range(QUAD // HEAD):
            scores = dot_nt(k * (masks[h] * (HEAD**-0.5)), q) + bias
            top = jnp.max(scores, axis=0, keepdims=True)
            grown = jnp.exp(scores - top)
            probs = (grown * (1.0 / jnp.sum(grown, axis=0, keepdims=True))).astype(BF)
            probs_ref[first + g * (QUAD // HEAD) + h] = probs
            part = dot_tn(probs, v * masks[h])
            total = part if total is None else total + part
        outs.append(total.astype(BF))
    return jnp.concatenate(outs, axis=1)


def attend_back(queries, keys, values, probs_ref, first, grad_mixed):
    masks = lane_masks()
    grads = []
    for g in range(D // QUAD):
        cols = slice(g * QUAD, (g + 1) * QUAD)
        q, k, v, go = queries[:, cols], keys[:, cols], values[:, cols], grad_mixed[:, cols]
        gq = gk = gv = None
        for h in range(QUAD // HEAD):
            probs_low = probs_ref[first + g * (QUAD // HEAD) + h]
            probs = probs_low.astype(F32)
            grad_probs = dot_nt(v * masks[h], go)
            both = probs * grad_probs
            grad_scores = (both - probs * jnp.sum(both, axis=0, keepdims=True)).astype(BF)
            part_v = dot(probs_low, go * masks[h])
            part_k = dot(grad_scores, q * masks[h])
            part_q = dot_tn(grad_scores, k * masks[h])
            gv = part_v if gv is None else gv + part_v
            gk = part_k if gk is None else gk + part_k
            gq = part_q if gq is None else gq + part_q
        grads.append((gq * (HEAD**-0.5), gk * (HEAD**-0.5), gv))
    return tuple(jnp.concatenate(parts, axis=1) for parts in zip(*grads))


def put_block(held, index, product):
    held[:, :, index * BLOCK : (index + 1) * BLOCK] = product.astype(BF).reshape(4, 4, BLOCK, D)


def self_forward_kernel(passes, row, offset, me_ref, lengths, gains, *refs):
    inputs, refs = refs[:passes], refs[passes:]
    pieces, refs = refs[:4], refs[4:]
    out_ref, normed_ref, joined_ref, probs_ref, mixed_ref, held, sems = refs
    loads = fetch(me_ref, pieces, offset, held, sems)
    for p in range(passes):
        rows = slice(p * TOK, (p + 1) * TOK)
        unit, unused = normed_of(inputs[p][...].astype(F32))
        normed_ref[rows] = (unit * gains[row : row + 1] + gains[row + 1 : row + 2]).astype(BF)
    wait_all(loads)
    for b in range(3):
        joined_ref[:, b * D : (b + 1) * D] = dot(normed_ref[...], column_block(held, b)).astype(BF)
    bias = mask_bias(lengths, lengths)
    for p in range(passes):
        rows = slice(p * TOK, (p + 1) * TOK)
        mixed = attend(
            joined_ref[rows, 0:D],
            joined_ref[rows, D : 2 * D],
            joined_ref[rows, 2 * D : 3 * D],
            bias,
            probs_ref,
            p * HEADS,
        )
        mixed_ref[rows] = mixed
        out_ref[rows] = inputs[p][...].astype(F32) + dot(mixed, column_block(held, 3))


def self_back_kernel(passes, row, offset, me_ref, gains, *refs):
    inputs, refs = refs[:passes], refs[passes:]
    grad_out, normed, joined, probs, mixed = refs[:5]
    pieces, refs = refs[5:9], refs[9:]
    grad_in, norm_ref, own, other, held, made, back, sems = refs
    loads = fetch(me_ref, pieces, offset, held, sems)
    grad_low = grad_out[...].astype(BF)
    put_block(made, 3, dot_tn(mixed[...], grad_low))
    wait_all(loads)
    grad_mixed = dot_nt(grad_low, column_block(held, 3)).astype(BF)
    for p in range(passes):
        rows = slice(p * TOK, (p + 1) * TOK)
        grads = attend_back(
            joined[rows, 0:D],
            joined[rows, D : 2 * D],
            joined[rows, 2 * D : 3 * D],
            probs,
            p * HEADS,
            grad_mixed[rows],
        )
        for b in range(3):
            back[rows, b * D : (b + 1) * D] = grads[b].astype(BF)
    grad_normed = None
    for b in range(3):
        part = back[:, b * D : (b + 1) * D]
        put_block(made, b, dot_tn(normed[...], part))
        step = dot_nt(part, column_block(held, b))
        grad_normed = step if grad_normed is None else grad_normed + step
    stores = deliver(me_ref, made, own, other, sems)
    units = [normed_of(inputs[p][...].astype(F32)) for p in range(passes)]
    unit = jnp.concatenate([u[0] for u in units], axis=0)
    inverse = jnp.concatenate([u[1] for u in units], axis=0)
    grad = norm_back(unit, inverse, gains[row : row + 1], grad_normed, norm_ref)
    grad_in[...] = grad_out[0:TOK] + grad[0:TOK]
    wait_all(stores)


def cross_forward_kernel(row, offset, me_ref, src_lengths, tgt_lengths, gains, hidden, memory, *refs):
    pieces, refs = refs[:4], refs[4:]
    out_ref, normed_ref, query_ref, pair_ref, probs_ref, mixed_ref, held, sems = refs
    loads = fetch(me_ref, pieces, offset, held, sems)
    unit, unused = normed_of(hidden[...])
    normed_ref[...] = (unit * gains[row : row + 1] + gains[row + 1 : row + 2]).astype(BF)
    wait_all(loads)
    query_ref[...] = dot(normed_ref[...], column_block(held, 0)).astype(BF)
    for b in range(2):
        pair_ref[:, b * D : (b + 1) * D] = dot(memory[...], column_block(held, 1 + b)).astype(BF)
    bias = mask_bias(src_lengths, tgt_lengths)
    for p in range(2):
        rows = slice(p * TOK, (p + 1) * TOK)
        mixed = attend(
            query_ref[rows], pair_ref[:, 0:D], pair_ref[:, D : 2 * D], bias, probs_ref, p * HEADS
        )
        mixed_ref[rows] = mixed
        out_ref[rows] = hidden[rows] + dot(mixed, column_block(held, 3))


def cross_back_kernel(row, offset, me_ref, gains, hidden, memory, grad_out, normed, query, pair, probs, mixed, *refs):
    pieces, refs = refs[:4], refs[4:]
    grad_in, grad_memory, norm_ref, own, other, held, made, back, sems = refs
    loads = fetch(me_ref, pieces, offset, held, sems)
    grad_low = grad_out[...].astype(BF)
    put_block(made, 3, dot_tn(mixed[...], grad_low))
    wait_all(loads)
    grad_mixed = dot_nt(grad_low, column_block(held, 3)).astype(BF)
    grad_key = grad_value = None
    for p in range(2):
        rows = slice(p * TOK, (p + 1) * TOK)
        grads = attend_back(
            query[rows], pair[:, 0:D], pair[:, D : 2 * D], probs, p * HEADS, grad_mixed[rows]
        )
        back[rows] = grads[0].astype(BF)
        grad_key = grads[1] if grad_key is None else grad_key + grads[1]
        grad_value = grads[2] if grad_value is None else grad_value + grads[2]
    grad_key = grad_key.astype(BF)
    grad_value = grad_value.astype(BF)
    put_block(made, 0, dot_tn(normed[...], back[...]))
    put_block(made, 1, dot_tn(memory[...], grad_key))
    put_block(made, 2, dot_tn(memory[...], grad_value))
    stores = deliver(me_ref, made, own, other, sems)
    grad_memory[...] = dot_nt(grad_key, column_block(held, 1)) + dot_nt(
        grad_value, column_block(held, 2)
    )
    grad_normed = dot_nt(back[...], column_block(held, 0))
    unit, inverse = normed_of(hidden[...])
    grad = norm_back(unit, inverse, gains[row : row + 1], grad_normed, norm_ref)
    grad_in[...] = grad_out[...] + grad
    wait_all(stores)


GELU_SCALE = 0.7978845608028654
GELU_CUBE = 0.044715


def gelu_both(up):
    square = up * up
    bent = jnp.tanh(GELU_SCALE * up * (1.0 + GELU_CUBE * square))
    half = 0.5 * (1.0 + bent)
    slope = half + 0.5 * up * (1.0 - bent * bent) * (
        GELU_SCALE * (1.0 + (3.0 * GELU_CUBE) * square)
    )
    return up * half, slope


def ffn_forward_kernel(row, offset, me_ref, gains, hidden, *refs):
    pieces, refs = refs[:4], refs[4:]
    memory, normed_ref, active_ref, slope_ref, held, sems = refs
    loads = fetch(me_ref, pieces, offset, held, sems)
    unit, unused = normed_of(hidden[...])
    normed_ref[...] = (unit * gains[row : row + 1] + gains[row + 1 : row + 2]).astype(BF)
    wait_all(loads)
    for b in range(4):
        cols = slice(b * D, (b + 1) * D)
        active, slope = gelu_both(dot(normed_ref[...], column_block(held, b)))
        active_ref[:, cols] = active.astype(BF)
        slope_ref[:, cols] = slope.astype(BF)
    total = hidden[...]
    for z in range(4):
        total = total + dot(active_ref[:, z * D : (z + 1) * D], row_block(held, z))
    memory[...] = total.astype(BF)


def ffn_back_kernel(row, offset, me_ref, gains, hidden, grad_out, normed, active, slope, *refs):
    pieces, refs = refs[:4], refs[4:]
    grad_in, norm_ref, own, other, held, made, sems = refs
    loads = fetch(me_ref, pieces, offset, held, sems)
    grad_low = grad_out[...].astype(BF)
    wait_all(loads)
    grad = ffn_back_core(gains[row : row + 1], hidden[...], grad_low, normed, active, slope, norm_ref, held, made)
    stores = deliver(me_ref, made, own, other, sems)
    grad_in[...] = grad_out[...] + grad
    wait_all(stores)


def ffn_back_core(gain, hidden, grad_low, normed, active, slope, norm_ref, held, made):
    grad_normed = None
    for b in range(4):
        cols = slice(b * D, (b + 1) * D)
        made[b, :, 4 * BLOCK : 8 * BLOCK] = dot_tn(active[:, cols], grad_low).astype(BF).reshape(4, 4 * BLOCK, D)
        grad_active = dot_nt(grad_low, row_block(held, b))
        grad_up = (slope[:, cols].astype(F32) * grad_active).astype(BF)
        put_block(made, b, dot_tn(normed[...], grad_up))
        step = dot_nt(grad_up, column_block(held, b))
        grad_normed = step if grad_normed is None else grad_normed + step
    unit, inverse = normed_of(hidden)
    return norm_back(unit, inverse, gain, grad_normed, norm_ref)


def ffn_both_kernel(row, offset, me_ref, gains, hidden, cot_first, cot_second, *refs):
    pieces, refs = refs[:4], refs[4:]
    first_out, second_out, grad_in, norm_ref, own, other, held, made, normed, active, slope, sems = refs
    loads = fetch(me_ref, pieces, offset, held, sems)
    unit, unused = normed_of(hidden[...])
    normed[...] = (unit * gains[row : row + 1] + gains[row + 1 : row + 2]).astype(BF)
    wait_all(loads)
    for b in range(4):
        cols = slice(b * D, (b + 1) * D)
        grown, bent = gelu_both(dot(normed[...], column_block(held, b)))
        active[:, cols] = grown.astype(BF)
        slope[:, cols] = bent.astype(BF)
    total = hidden[...]
    for z in range(4):
        total = total + dot(active[:, z * D : (z + 1) * D], row_block(held, z))
    first_out[...] = total[0:TOK].astype(BF)
    second_out[...] = total[TOK:].astype(BF)
    grad_low = jnp.concatenate([cot_first[...], cot_second[...]], axis=0)
    grad = ffn_back_core(gains[row : row + 1], hidden[...], grad_low, normed, active, slope, norm_ref, held, made)
    stores = deliver(me_ref, made, own, other, sems)
    grad_in[...] = grad_low.astype(F32) + grad
    wait_all(stores)


ANY = pl.BlockSpec(memory_space=pl.ANY)
VM = pl.BlockSpec(memory_space=pltpu.VMEM)
SM = pl.BlockSpec(memory_space=pltpu.SMEM)


def held_of(blocks):
    return pltpu.VMEM((4, 4, blocks * BLOCK, D), BF)


def halves(blocks):
    return [jax.ShapeDtypeStruct((2, 2, 4, 2, blocks * BLOCK // 4, D), BF)] * 2


def shape(rows, cols, dtype):
    return jax.ShapeDtypeStruct((rows, cols), dtype)


def call(body, name, in_specs, out_shape, out_specs, scratch, operands, gflop):
    return pl.pallas_call(
        body,
        name=name,
        out_shape=out_shape,
        in_specs=in_specs,
        out_specs=out_specs,
        scratch_shapes=scratch,
        compiler_params=pltpu.CompilerParams(vmem_limit_bytes=VMEM_LIMIT),
        cost_estimate=pl.CostEstimate(
            flops=int(gflop * 1e8), bytes_accessed=1 << 20, transcendentals=1 << 10
        ),
    )(*operands)


def self_forward(row, me, lengths, gains, inputs, pieces):
    count = len(inputs)
    rows = count * TOK
    return call(
        functools.partial(self_forward_kernel, count, row, pieces[0]),
        "self_forward",
        [SM, SM, VM] + [VM] * count + [ANY] * 4,
        [
            shape(rows, D, F32),
            shape(rows, D, BF),
            shape(rows, 3 * D, BF),
            jax.ShapeDtypeStruct((count * HEADS, TOK, TOK), BF),
            shape(rows, D, BF),
        ],
        [VM] * 5,
        [held_of(4), pltpu.SemaphoreType.DMA((32,))],
        (me, lengths, gains, *inputs, *pieces[1]),
        2 * count,
    )


def self_back(row, me, gains, inputs, grad_out, kept, pieces):
    count = len(inputs)
    rows = count * TOK
    return call(
        functools.partial(self_back_kernel, count, row, pieces[0]),
        "self_back",
        [SM, VM] + [VM] * count + [VM] * 5 + [ANY] * 4,
        [shape(TOK, D, F32), shape(2, D, F32)] + halves(4),
        [VM, VM, ANY, ANY],
        [held_of(4), held_of(4), pltpu.VMEM((rows, 3 * D), BF), pltpu.SemaphoreType.DMA((32,))],
        (me, gains, *inputs, grad_out, *kept, *pieces[1]),
        4 * count,
    )


def cross_forward(row, me, src_lengths, tgt_lengths, gains, hidden, memory, pieces):
    return call(
        functools.partial(cross_forward_kernel, row, pieces[0]),
        "cross_forward",
        [SM, SM, SM, VM, VM, VM] + [ANY] * 4,
        [
            shape(2 * TOK, D, F32),
            shape(2 * TOK, D, BF),
            shape(2 * TOK, D, BF),
            shape(TOK, 2 * D, BF),
            jax.ShapeDtypeStruct((2 * HEADS, TOK, TOK), BF),
            shape(2 * TOK, D, BF),
        ],
        [VM] * 6,
        [held_of(4), pltpu.SemaphoreType.DMA((32,))],
        (me, src_lengths, tgt_lengths, gains, hidden, memory, *pieces[1]),
        3,
    )


def cross_back(row, me, gains, hidden, memory, grad_out, kept, pieces):
    return call(
        functools.partial(cross_back_kernel, row, pieces[0]),
        "cross_back",
        [SM] + [VM] * 9 + [ANY] * 4,
        [shape(2 * TOK, D, F32), shape(TOK, D, F32), shape(2, D, F32)] + halves(4),
        [VM, VM, VM, ANY, ANY],
        [held_of(4), held_of(4), pltpu.VMEM((2 * TOK, D), BF), pltpu.SemaphoreType.DMA((32,))],
        (me, gains, hidden, memory, grad_out, *kept, *pieces[1]),
        6,
    )


def ffn_forward(row, me, gains, hidden, pieces):
    return call(
        functools.partial(ffn_forward_kernel, row, pieces[0]),
        "ffn_forward",
        [SM, VM, VM] + [ANY] * 4,
        [shape(TOK, D, BF), shape(TOK, D, BF), shape(TOK, FF, BF), shape(TOK, FF, BF)],
        [VM] * 4,
        [held_of(8), pltpu.SemaphoreType.DMA((32,))],
        (me, gains, hidden, *pieces[1]),
        2,
    )


def ffn_back(row, me, gains, hidden, grad_out, kept, pieces):
    return call(
        functools.partial(ffn_back_kernel, row, pieces[0]),
        "ffn_back",
        [SM, VM, VM, VM, VM, VM, VM] + [ANY] * 4,
        [shape(TOK, D, F32), shape(2, D, F32)] + halves(8),
        [VM, VM, ANY, ANY],
        [held_of(8), held_of(8), pltpu.SemaphoreType.DMA((32,))],
        (me, gains, hidden, grad_out, *kept, *pieces[1]),
        4,
    )


def ffn_both(row, me, gains, hidden, cot_first, cot_second, pieces):
    rows = 2 * TOK
    return call(
        functools.partial(ffn_both_kernel, row, pieces[0]),
        "ffn_both",
        [SM, VM, VM, VM, VM] + [ANY] * 4,
        [shape(TOK, D, BF), shape(TOK, D, BF), shape(rows, D, F32), shape(2, D, F32)] + halves(8),
        [VM, VM, VM, VM, ANY, ANY],
        [
            held_of(8),
            held_of(8),
            pltpu.VMEM((rows, D), BF),
            pltpu.VMEM((rows, FF), BF),
            pltpu.VMEM((rows, FF), BF),
            pltpu.SemaphoreType.DMA((32,)),
        ],
        (me, gains, hidden, cot_first, cot_second, *pieces[1]),
        9,
    )


AXIS = "fsdp"
BOTH = ("dp", "fsdp")
SHARDS = 16


def route(target):
    pairs = []
    for i in range(2 * SHARDS):
        dp, z, y, core = target(i // 16, (i // 4) % 4, (i // 2) % 2, i % 2)
        pairs.append((i, dp * 16 + (z % 4) * 4 + y * 2 + core))
    return pairs


def to_core(x):
    return lax.ppermute(x, BOTH, route(lambda dp, z, y, core: (dp, z, y, 1 - core)))


def to_z(x, step):
    return lax.ppermute(x, BOTH, route(lambda dp, z, y, core: (dp, z + step, y, core)))


def to_y(x):
    return lax.ppermute(x, BOTH, route(lambda dp, z, y, core: (dp, z, 1 - y, core)))


def to_dp(x):
    return lax.ppermute(x, BOTH, route(lambda dp, z, y, core: (1 - dp, z, y, core)))


def to_yx(x):
    return lax.ppermute(
        x, BOTH, route(lambda dp, z, y, core: (dp, z, y ^ 1, core) if core == 0 else (dp ^ 1, z, y, core))
    )


def to_xy(x):
    return lax.ppermute(
        x, BOTH, route(lambda dp, z, y, core: (dp ^ 1, z, y, core) if core == 0 else (dp, z, y ^ 1, core))
    )


def after(value, *earlier):
    return lax.optimization_barrier((value,) + tuple(earlier))[0]


def blocks_of(shard):
    rows, cols = shard.shape
    split = shard.reshape(rows // BLOCK, BLOCK, cols // D, D)
    return split.transpose(2, 0, 1, 3).reshape(-1, BLOCK, D)


def shard_of(blocks, cols):
    wide = blocks.reshape(cols // D, -1, D)
    return wide.transpose(1, 0, 2).reshape(-1, cols)


def quarters_of(weights):
    blocks = jnp.concatenate([blocks_of(weight) for weight in weights])
    return blocks.reshape(4, -1, D)


def as_pair(core, own, came):
    return jnp.where(core == 0, jnp.stack([own, came]), jnp.stack([came, own]))


class Gather:
    def __init__(self, place, chunk):
        core, half = place[3], place[2]
        mine = lax.dynamic_slice_in_dim(chunk, 2 * half, 2, 0)
        own = jnp.where(core == 0, mine[0], mine[1])
        other = jnp.where(core == 0, mine[1], mine[0])
        self.pair = as_pair(core, own, to_core(other))

    def along_z(self):
        self.line = jnp.stack([self.pair] + [to_z(self.pair, d) for d in (1, 2, 3)])

    def first_cross(self):
        self.both = jnp.stack([self.line, to_xy(self.line)])

    def second_cross(self):
        came = to_yx(self.both)
        self.pieces = (self.both, came, to_core(self.both), to_core(came))


def gather_norms(place, rows):
    block = jnp.pad(rows, ((0, 6), (0, D - rows.shape[1])))
    pair = as_pair(place[3], block, to_core(block))
    line = jnp.stack([pair] + [to_z(pair, d) for d in (1, 2, 3)])
    across = to_y(line)
    both = jnp.where(place[1] == 0, jnp.stack([line, across]), jnp.stack([across, line]))
    both = both[:, :, :, 0:10, 0:BLOCK]
    turned = jnp.concatenate([both, both], axis=1)
    ordered = lax.dynamic_slice_in_dim(turned[:, ::-1], 3 - place[0], 4, 1)
    return ordered[:, ::1].transpose(3, 1, 0, 2, 4).reshape(10, D)


class Reduce:
    def __init__(self):
        self.parts = []

    def add(self, own, other):
        self.parts.append((own, to_core(other)))

    def first(self):
        sums = [(own.astype(F32) + came.astype(F32)).astype(BF) for own, came in self.parts]
        self.keep = jnp.concatenate([part[0] for part in sums], axis=3)
        self.came = to_yx(jnp.concatenate([part[1] for part in sums], axis=3))

    def second(self):
        total = (self.keep.astype(F32) + self.came.astype(F32)).astype(BF)
        self.keep = total[0]
        self.came = to_xy(total[1])

    def along_z(self):
        total = (self.keep.astype(F32) + self.came.astype(F32)).astype(BF)
        self.keep = [total[0]] + [to_z(total[d], d) for d in (1, 2, 3)]

    def last(self, place):
        total = self.keep[0].astype(F32)
        for part in self.keep[1:]:
            total = total + part.astype(F32)
        total = total.astype(BF)
        core, half = place[3], place[2]
        own = jnp.where(core == 0, total[0], total[1])
        other = jnp.where(core == 0, total[1], total[0])
        pair = as_pair(core, own, to_core(other))
        self.ends = (pair, to_dp(pair))

    def shard(self, place):
        pair, came = self.ends
        whole = jnp.where(
            place[2] == 0, jnp.concatenate([pair, came]), jnp.concatenate([came, pair])
        )
        return whole.astype(F32)


def reduce_norms(place, rows):
    total = jnp.pad(rows, ((0, 6), (0, 0)))
    for move in (to_core, to_y):
        total = total + move(total)
    total = total + to_z(total, 1) + to_z(total, 2) + to_z(total, 3)
    total = total + to_dp(total)
    spot = place[0] * 4 + place[1] * 2 + place[3]
    return lax.dynamic_slice_in_dim(total, spot * BLOCK, BLOCK, 1)[0:10]


def gather_plain(weights):
    parts = []
    for weight in weights:
        whole = lax.all_gather(weight, AXIS, axis=0, tiled=True)
        shards = whole.reshape(SHARDS, -1, whole.shape[1])
        parts.append(jax.vmap(blocks_of)(shards))
    chunk = jnp.concatenate(parts, axis=1).reshape(4, 2, 2, 2, 2, -1, D)
    chunk = jnp.concatenate([chunk[0:1], chunk[:0:-1]], axis=0)
    pieces = []
    for first in range(2):
        pieces.append(chunk[:, first, :, :, 0].transpose(2, 0, 1, 3, 4))
    for first in range(2):
        pieces.append(chunk[:, :, :, first, 1].transpose(1, 0, 2, 3, 4))
    return tuple(pieces)


def reduce_plain(own, other, columns):
    sets = jnp.stack([own.transpose(2, 0, 3, 1, 4, 5), other.transpose(2, 1, 3, 0, 4, 5)], axis=4)
    shards = sets.reshape(SHARDS, -1, BLOCK, D)
    grads = []
    for first, last, cols in columns:
        whole = jax.vmap(functools.partial(shard_of, cols=cols))(shards[:, first:last])
        whole = whole.reshape(-1, cols).astype(F32)
        part = lax.psum_scatter(whole, AXIS, scatter_dimension=0, tiled=True)
        grads.append(lax.psum(part.astype(BF), "dp").astype(F32))
    return grads


def norm_rows_of(gain_enc, bias_enc, gain_dec, bias_dec):
    rows = []
    for gain, bias in ((gain_enc, bias_enc), (gain_dec, bias_dec)):
        for k in range(gain.shape[0]):
            rows += [gain[k : k + 1], bias[k : k + 1]]
    return jnp.concatenate(rows, axis=0)


ATTN_COLUMNS = ((0, 3, 3 * D), (3, 4, D))
FFN_COLUMNS = ((0, 4, FF), (4, 8, D))
CROSS_COLUMNS = ((0, 1, D), (1, 3, 2 * D), (3, 4, D))


def shards_of(group, columns):
    blocks = group.reshape(-1, BLOCK, D)
    return [shard_of(blocks[first:last], cols) for first, last, cols in columns]


def step(
    custom,
    source,
    first_in,
    second_in,
    cot_first,
    cot_second,
    src_lengths,
    tgt_lengths,
    enc_attn_in,
    enc_attn_out,
    enc_ffn_in,
    enc_ffn_out,
    enc_gain,
    enc_bias,
    dec_self_in,
    dec_self_out,
    dec_cross_q,
    dec_cross_kv,
    dec_cross_out,
    dec_ffn_in,
    dec_ffn_out,
    dec_gain,
    dec_bias,
):
    spot = lax.axis_index(AXIS)
    norm_rows = norm_rows_of(enc_gain, enc_bias, dec_gain, dec_bias)
    group_self = (dec_self_in, dec_self_out)
    group_enc = (enc_attn_in, enc_attn_out)
    group_enc_ffn = (enc_ffn_in, enc_ffn_out)
    group_cross = (dec_cross_q, dec_cross_kv, dec_cross_out)
    group_ffn = (dec_ffn_in, dec_ffn_out)
    if custom:
        place = jnp.stack([spot >> 2, (spot >> 1) & 1, lax.axis_index("dp"), spot & 1]).astype(jnp.int32)
        chunk_a = jnp.concatenate([quarters_of(group_self), quarters_of(group_enc)], axis=1)
        chunk_b = jnp.concatenate([quarters_of(group_enc_ffn), quarters_of(group_cross)], axis=1)
        chunk_c = quarters_of(group_ffn)
        one = Gather(place, chunk_a)
        one.along_z()
        norms = gather_norms(place, after(norm_rows, one.pair))
        two = Gather(place, chunk_b)
        two.pair = after(two.pair, one.line)
        one.first_cross()
        two.along_z()
        one.second_cross()
        two.line = after(two.line, one.pieces[1])
        three = Gather(place, chunk_c)
        three.pair = after(three.pair, two.line)
        three.along_z()
        two.first_cross()
        two.second_cross()
        three.line = after(three.line, two.pieces[1])
        three.first_cross()
        three.second_cross()
        w_self, w_enc = (0, one.pieces), (32, one.pieces)
        w_enc_ffn, w_cross = (0, two.pieces), (64, two.pieces)
        w_ffn = (0, three.pieces)
    else:
        place = jnp.zeros((4,), jnp.int32)
        w_self, w_enc, w_enc_ffn, w_cross, w_ffn = (
            (0, gather_plain(group))
            for group in (group_self, group_enc, group_enc_ffn, group_cross, group_ffn)
        )
        norms = lax.all_gather(norm_rows, AXIS, axis=1, tiled=True)
    gains = jnp.pad(norms.astype(F32), ((0, 6), (0, 0)))

    hidden_one, *kept_self = self_forward(4, place, tgt_lengths, gains, [first_in, second_in], w_self)
    hidden_enc, *kept_enc = self_forward(0, place, src_lengths, gains, [source], w_enc)
    memory, *kept_enc_ffn = ffn_forward(2, place, gains, hidden_enc, w_enc_ffn)
    hidden_two, *kept_cross = cross_forward(
        6, place, src_lengths, tgt_lengths, gains, hidden_one, memory, w_cross
    )
    first_out, second_out, grad_two, norm_ffn, *made_ffn = ffn_both(
        8, place, gains, hidden_two, cot_first, cot_second, w_ffn
    )
    if custom:
        red_one, red_two, red_three = Reduce(), Reduce(), Reduce()
        red_one.add(*made_ffn)
    grad_one, grad_memory, norm_cross, *made_cross = cross_back(
        6, place, gains, hidden_one, memory, grad_two, kept_cross, w_cross
    )
    if custom:
        red_two.add(*made_cross)
        red_one.first()
        grad_memory = after(grad_memory, red_one.keep)
    grad_enc, norm_enc_ffn, *made_enc_ffn = ffn_back(
        2, place, gains, hidden_enc, grad_memory, kept_enc_ffn, w_enc_ffn
    )
    if custom:
        red_two.add(*made_enc_ffn)
        grad_one = after(grad_one, grad_enc)
    grad_first, norm_self, *made_self = self_back(
        4, place, gains, [first_in, second_in], grad_one, kept_self, w_self
    )
    if custom:
        red_three.add(*made_self)
        red_one.second()
        red_two.first()
        grad_enc = after(grad_enc, grad_first, red_one.keep, red_two.keep)
    grad_source, norm_enc, *made_enc = self_back(
        0, place, gains, [source], grad_enc, kept_enc, w_enc
    )
    norm_grads = jnp.concatenate([norm_enc, norm_enc_ffn, norm_self, norm_cross, norm_ffn], axis=0)
    if custom:
        red_three.add(*made_enc)
        red_one.along_z()
        red_two.second()
        red_three.first()
        red_one.last(place)
        red_two.along_z()
        red_three.second()
        red_two.last(place)
        red_three.along_z()
        red_three.last(place)
        norm_shard = reduce_norms(place, norm_grads)
        shard_one, shard_two, shard_three = (
            red.shard(place) for red in (red_one, red_two, red_three)
        )
        grads_ffn = shards_of(shard_one, FFN_COLUMNS)
        grads_cross = shards_of(shard_two[:, 0:32], CROSS_COLUMNS)
        grads_enc_ffn = shards_of(shard_two[:, 32:96], FFN_COLUMNS)
        grads_self = shards_of(shard_three[:, 0:32], ATTN_COLUMNS)
        grads_enc = shards_of(shard_three[:, 32:64], ATTN_COLUMNS)
    else:
        grads_ffn = reduce_plain(*made_ffn, FFN_COLUMNS)
        grads_cross = reduce_plain(*made_cross, CROSS_COLUMNS)
        grads_enc_ffn = reduce_plain(*made_enc_ffn, FFN_COLUMNS)
        grads_self = reduce_plain(*made_self, ATTN_COLUMNS)
        grads_enc = reduce_plain(*made_enc, ATTN_COLUMNS)
        norm_shard = lax.psum_scatter(norm_grads, AXIS, scatter_dimension=1, tiled=True)
        norm_shard = lax.psum(norm_shard.astype(BF), "dp").astype(F32)
    return (
        first_out,
        second_out,
        grad_source,
        grad_first,
        *grads_enc,
        *grads_enc_ffn,
        norm_shard[0:4:2],
        norm_shard[1:4:2],
        *grads_self,
        *grads_cross,
        *grads_ffn,
        norm_shard[4:10:2],
        norm_shard[5:10:2],
    )


def solution(mesh):
    blocked = P(("dp", "fsdp"), None)
    rows = P("fsdp", None)
    columns = P(None, "fsdp")
    custom = mesh.shape["fsdp"] == SHARDS and mesh.shape["dp"] == 2
    return jax.shard_map(
        functools.partial(step, custom),
        mesh=mesh,
        in_specs=(blocked,) * 7 + (rows,) * 4 + (columns,) * 2 + (rows,) * 7 + (columns,) * 2,
        out_specs=(blocked,) * 4 + (rows,) * 4 + (columns,) * 2 + (rows,) * 7 + (columns,) * 2,
        check_vma=False,
    )
```

time: 1450 us -> 353 us (0.24)
  waiting for transfers between devices: 1010 us -> 163 us
  blocking collectives: 164 us -> 0 us
  matrix products: 127 us -> 0 us
  Pallas kernels: 0 us -> 88.7 us
  starting transfers between devices: 1.14 us -> 57.8 us
  local copies, waits for them, and re-layouts: 67.1 us -> 16.2 us
  other arithmetic: 59.1 us -> 21.4 us
  between operations: 16.8 us -> 2.09 us
    reduce_scatter x11 -> x0, waiting for transfers between devices: 726 us -> none  [the longest x1 74.1 us: body(): lax.psum_scatter(enc_grads[2], 'fsdp', scatter_dimension=0, tiled=True)]
    unnamed x28 -> x0, waiting for transfers between devices: 177 us -> none
    all_gather x8 -> x0, blocking collectives: 164 us -> none  [the longest x1 23.4 us: body(): lax.all_gather(dec_bias, 'fsdp', axis=1, tiled=True)]
    ppermute x0 -> x61, waiting for transfers between devices: none -> 163 us  [the longest x24 73.2 us: to_z(): lax.ppermute(x, BOTH, route(lambda dp, z, y, core: (dp, z + step, y, core)))]
    dot_general x83 -> x0, matrix products: 127 us -> none  [the longest x18 33.8 us: contract_rows(): lax.dot_general(left, right, (((0,), (0,)), ((), ())), preferred_element_...]
    pallas_call x0 -> x9, Pallas kernels: none -> 88.7 us  [call(): pl.pallas_call(body, name=name, out_shape=out_shape, in_specs=in_specs, o...]
    ppermute x0 -> x61, starting transfers between devices: none -> 57.8 us  [the longest x24 30.1 us: to_z(): lax.ppermute(x, BOTH, route(lambda dp, z, y, core: (dp, z + step, y, core)))]
    all_gather x7 -> x0, waiting for transfers between devices: 56.3 us -> none  [the longest x1 36.4 us: body(): lax.all_gather(dec_ffn_in, 'fsdp', axis=0, tiled=True)]
  transfers between devices with their start and end apart: 24 -> 61, of which waited for: 19 -> 39; matrix products, arithmetic and copies ran while one was open for 10% -> 8% of each run, Pallas kernels for 0% -> 8%
where the time goes in v1:
time: 353 us; the launch traced here: 349 us
  waiting for transfers between devices  163 us (46%)
  Pallas kernels  88.7 us (25%)
  starting transfers between devices  57.8 us (16%)
  other arithmetic  21.4 us (6%)
  local copies, waits for them, and re-layouts  16.2 us (5%)
    pallas_call x9, Pallas kernels, call(): pl.pallas_call(body, name=name, out_shape=out_shape, in_specs=in_specs, o...  88.7 us
    ppermute x24, waiting for transfers between devices, to_z(): lax.ppermute(x, BOTH, route(lambda dp, z, y, core: (dp, z + step, y, core)))  73.2 us
    ppermute x6, waiting for transfers between devices, to_xy(): lax.ppermute(x, BOTH, route(lambda dp, z, y, core: (dp ^ 1, z, y, core) i...  31.2 us
    ppermute x24, starting transfers between devices, to_z(): lax.ppermute(x, BOTH, route(lambda dp, z, y, core: (dp, z + step, y, core)))  30.1 us
    ppermute x6, waiting for transfers between devices, to_yx(): lax.ppermute(x, BOTH, route(lambda dp, z, y, core: (dp, z, y ^ 1, core) i...  23.6 us
    ppermute x2, waiting for transfers between devices, to_y(): lax.ppermute(x, BOTH, route(lambda dp, z, y, core: (dp, z, 1 - y, core)))  14.6 us
    ppermute x19, waiting for transfers between devices, to_core(): lax.ppermute(x, BOTH, route(lambda dp, z, y, core: (dp, z, y, 1 - core)))  13.2 us
    convert_element_type x5, other arithmetic, first(): (own.astype(F32) + came.astype(F32)).astype(BF)  8.74 us
  transfers between devices with their start and end apart: 61, of which 39 were waited for; matrix products, arithmetic and copies ran while one was open for 8% of the time, Pallas kernels for 8%

profile of v1, /device:TPU:0, one launch (start us, length us, event | category | flops | bytes accessed | tf_op | source)
XLA Modules:
  0.0 348.9 jit_solution(16478646601323068121)
XLA Ops:
  5.0 5.0 %collective-permute-start.8 = (bf16[2,64,512]{2,1,0:T(8,128)(2,1)S(1)}, bf16[2,64,512]{2,1,0:T(8,128)(2,1)S(1)}, u32[]{:S(2)}, u32[]{:S(2)}) collective-permute-start(bf16[2,64,512]{2,1,0:T(8,128)(2,1)S(1)} %maximum_select_fusion.5), channel_id=1, source_target_pairs={{0,12},{1,13},{2,14},{3,15},{4,0},{5,1},{6,2},{7,3},{8,4},{9,5},{1... | collective-permute-start | bytes 393224 | tf_op jit(solution)/shard_map/ppermute | solution.py:547
  11.0 2.9 collective-permute-done.8
  13.9 7.8 %collective-permute-done.7 = bf16[2,64,512]{2,1,0:T(8,128)(2,1)S(1)} collective-permute-done((bf16[2,64,512]{2,1,0:T(8,128)(2,1)S(1)}, bf16[2,64,512]{2,1,0:T(8,128)(2,1)S(1)}, u32[]{:S(2)}, u32[]{:S(2)}) %collective-permute-start.7) | collective-permute-done | bytes 131104 | tf_op jit(solution)/shard_map/ppermute | solution.py:547
  21.8 1.6 collective-permute-start.9
  23.4 7.7 %collective-permute-done.9 = bf16[4,2,64,512]{3,2,1,0:T(8,128)(2,1)S(1)} collective-permute-done((bf16[4,2,64,512]{3,2,1,0:T(8,128)(2,1)S(1)}, bf16[4,2,64,512]{3,2,1,0:T(8,128)(2,1)S(1)}, u32[]{:S(2)}, u32[]{:S(2)}) %collective-permute-start.9) | collective-permute-done | bytes 524320 | tf_op jit(solution)/shard_map/ppermute | solution.py:565
  31.2 1.6 collective-permute-start.10
  37.2 1.9 collective-permute-start.14
  39.1 2.5 collective-permute-done.16
  41.6 13.4 %collective-permute-done.15 = bf16[2,96,512]{2,1,0:T(8,128)(2,1)S(1)} collective-permute-done((bf16[2,96,512]{2,1,0:T(8,128)(2,1)S(1)}, bf16[2,96,512]{2,1,0:T(8,128)(2,1)S(1)}, u32[]{:S(2)}, u32[]{:S(2)}) %collective-permute-start.15) | collective-permute-done | bytes 196640 | tf_op jit(solution)/shard_map/ppermute | solution.py:547
  55.1 1.6 collective-permute-start.17
  56.7 10.5 %collective-permute-done.17 = bf16[4,2,96,512]{3,2,1,0:T(8,128)(2,1)S(1)} collective-permute-done((bf16[4,2,96,512]{3,2,1,0:T(8,128)(2,1)S(1)}, bf16[4,2,96,512]{3,2,1,0:T(8,128)(2,1)S(1)}, u32[]{:S(2)}, u32[]{:S(2)}) %collective-permute-start.17) | collective-permute-done | bytes 786464 | tf_op jit(solution)/shard_map/ppermute | solution.py:565
  69.5 1.7 collective-permute-start.23
  71.2 1.9 collective-permute-start.22
  73.2 2.4 collective-permute-done.24
  75.6 7.8 %collective-permute-done.23 = bf16[2,64,512]{2,1,0:T(8,128)(2,1)S(1)} collective-permute-done((bf16[2,64,512]{2,1,0:T(8,128)(2,1)S(1)}, bf16[2,64,512]{2,1,0:T(8,128)(2,1)S(1)}, u32[]{:S(2)}, u32[]{:S(2)}) %collective-permute-start.23) | collective-permute-done | bytes 131104 | tf_op jit(solution)/shard_map/ppermute | solution.py:547
  83.5 4.5 %collective-permute-done.18.refs_1_ = bf16[2,4,2,96,512]{4,3,2,1,0:T(8,128)(2,1)} collective-permute-done((bf16[2,4,2,96,512]{4,3,2,1,0:T(8,128)(2,1)S(1)}, bf16[2,4,2,96,512]{4,3,2,1,0:T(8,128)(2,1)}, u32[]{:S(2)}, u32[]{:S(2)}) %collective-permute-start.18) | collective-permute-done | bytes 1572896 | tf_op jit(solution)/shard_map/ppermute | solution.py:559
  89.4 7.7 %collective-permute-done.25 = bf16[4,2,64,512]{3,2,1,0:T(8,128)(2,1)S(1)} collective-permute-done((bf16[4,2,64,512]{3,2,1,0:T(8,128)(2,1)S(1)}, bf16[4,2,64,512]{3,2,1,0:T(8,128)(2,1)S(1)}, u32[]{:S(2)}, u32[]{:S(2)}) %collective-permute-start.25) | collective-permute-done | bytes 524320 | tf_op jit(solution)/shard_map/ppermute | solution.py:565
  100.1 3.9 %collective-permute-done.4 = bf16[2,16,512]{2,1,0:T(8,128)(2,1)S(1)} collective-permute-done((bf16[2,16,512]{2,1,0:T(8,128)(2,1)S(1)}, bf16[2,16,512]{2,1,0:T(8,128)(2,1)S(1)}, u32[]{:S(2)}, u32[]{:S(2)}) %collective-permute-start.4) | collective-permute-done | bytes 32800 | tf_op jit(solution)/shard_map/ppermute | solution.py:547
  104.0 1.6 collective-permute-start.3
  105.6 3.2 collective-permute-done.3
  109.4 5.6 %collective-permute-done.2 = bf16[2,16,512]{2,1,0:T(8,128)(2,1)S(1)} collective-permute-done((bf16[2,16,512]{2,1,0:T(8,128)(2,1)S(1)}, bf16[2,16,512]{2,1,0:T(8,128)(2,1)S(1)}, u32[]{:S(2)}, u32[]{:S(2)}) %collective-permute-start.2) | collective-permute-done | bytes 32800 | tf_op jit(solution)/shard_map/ppermute | solution.py:547
  115.0 1.6 collective-permute-start.5
  116.6 3.4 collective-permute-done.5
  122.1 2.4 collective-permute-done.12.refs_5_.refs_4_.refs_10_.refs_9_
  124.5 5.8 %self_forward.3 = (f32[256,512]{1,0:T(8,128)}, bf16[256,512]{1,0:T(8,128)(2,1)}, bf16[256,1536]{1,0:T(8,128)(2,1)}, bf16[8,256,256]{2,1,0:T(8,128)(2,1)}, bf16[256,512]{1,0:T(8,128)(2,1)}) custom-call(s32[4]{0:T(128)} %pad_add_fusion.me_ref, s32[1,8]{1,0:T(1,128)} %src_lengths.1, f32[16,512]{1,0:T(8,128)} %pad_convert_fusion.gains, ...), custom_call_target="tpu_custom_call" | custom-call | flops 200000000 | bytes 1048576 | tf_op jit(solution)/shard_map/self_forward/pallas_call | solution.py:399
  130.3 8.3 %self_forward.2 = (f32[512,512]{1,0:T(8,128)}, bf16[512,512]{1,0:T(8,128)(2,1)}, bf16[512,1536]{1,0:T(8,128)(2,1)}, bf16[16,256,256]{2,1,0:T(8,128)(2,1)}, bf16[512,512]{1,0:T(8,128)(2,1)}) custom-call(s32[4]{0:T(128)} %pad_add_fusion.me_ref, s32[1,8]{1,0:T(1,128)} %tgt_lengths.1, f32[16,512]{1,0:T(8,128)} %pad_convert_fusion.gains, ...), custom_call_target="tpu_custom_call" | custom-call | flops 400000000 | bytes 1048576 | tf_op jit(solution)/shard_map/self_forward/pallas_call | solution.py:399
  138.6 6.6 %ffn_forward.1 = (bf16[256,512]{1,0:T(8,128)(2,1)}, bf16[256,512]{1,0:T(8,128)(2,1)}, bf16[256,2048]{1,0:T(8,128)(2,1)}, bf16[256,2048]{1,0:T(8,128)(2,1)}) custom-call(s32[4]{0:T(128)} %pad_add_fusion.me_ref, f32[16,512]{1,0:T(8,128)} %pad_convert_fusion.gains, f32[256,512]{1,0:T(8,128)} %get-tuple-element.72.hidden, bf16[2,4,2,96,512]{4,3,2,1,0:T(8,128)(2,1)} %copy-done, ...), custom_call_target="tpu_custom_call" | custom-call | flops 200000000 | bytes 1048576 | tf_op jit(solution)/shard_map/ffn_forward/pallas_call | solution.py:399
  145.2 7.9 %cross_forward.1 = (f32[512,512]{1,0:T(8,128)}, bf16[512,512]{1,0:T(8,128)(2,1)}, bf16[512,512]{1,0:T(8,128)(2,1)}, bf16[256,1024]{1,0:T(8,128)(2,1)}, bf16[16,2...) custom-call(s32[4]{0:T(128)} %pad_add_fusion.me_ref, s32[1,8]{1,0:T(1,128)} %src_lengths.1, s32[1,8]{1,0:T(1,128)} %tgt_lengths.1, ...), custom_call_target="tpu_custom_call" | custom-call | flops 300000000 | bytes 1048576 | tf_op jit(solution)/shard_map/cross_forward/pallas_call | solution.py:399
  154.1 15.5 %ffn_both.1 = (bf16[256,512]{1,0:T(8,128)(2,1)}, bf16[256,512]{1,0:T(8,128)(2,1)}, f32[512,512]{1,0:T(8,128)}, f32[2,512]{1,0:T(2,128)}, bf16[2,2,4,2,64,512]{5,...) custom-call(s32[4]{0:T(128)} %pad_add_fusion.me_ref, f32[16,512]{1,0:T(8,128)} %pad_convert_fusion.gains, ...), custom_call_target="tpu_custom_call" | custom-call | flops 900000000 | bytes 1048576 | tf_op jit(solution)/shard_map/ffn_both/pallas_call | solution.py:399
  169.7 12.5 %cross_back.1 = (f32[512,512]{1,0:T(8,128)}, f32[256,512]{1,0:T(8,128)}, f32[2,512]{1,0:T(2,128)}, bf16[2,2,4,2,32,512]{5,4,3,2,1,0:T(8,128)(2,1)}, bf16[2,2,4,2,32,512]{5,4,3,2,1,0:T(8,128)(2,1)}) custom-call(s32[4]{0:T(128)} %pad_add_fusion.me_ref, f32[16,512]{1,0:T(8,128)} %pad_convert_fusion.gains, f32[512,512]{1,0:T(8,128)} %get-tuple-element.71.hidden, ...), custom_call_target="tpu_custom_call" | custom-call | flops 600000000 | bytes 1048576 | tf_op jit(solution)/shard_map/cross_back/pallas_call | solution.py:399
  182.2 10.1 %ffn_back.1 = (f32[256,512]{1,0:T(8,128)}, f32[2,512]{1,0:T(2,128)}, bf16[2,2,4,2,64,512]{5,4,3,2,1,0:T(8,128)(2,1)}, bf16[2,2,4,2,64,512]{5,4,3,2,1,0:T(8,128)(2,1)}) custom-call(s32[4]{0:T(128)} %pad_add_fusion.me_ref, f32[16,512]{1,0:T(8,128)} %pad_convert_fusion.gains, f32[256,512]{1,0:T(8,128)} %get-tuple-element.72.hidden, ...), custom_call_target="tpu_custom_call" | custom-call | flops 400000000 | bytes 1048576 | tf_op jit(solution)/shard_map/ffn_back/pallas_call | solution.py:399
  192.3 12.6 %self_back.2 = (f32[256,512]{1,0:T(8,128)}, f32[2,512]{1,0:T(2,128)}, bf16[2,2,4,2,32,512]{5,4,3,2,1,0:T(8,128)(2,1)}, bf16[2,2,4,2,32,512]{5,4,3,2,1,0:T(8,128)(2,1)}) custom-call(s32[4]{0:T(128)} %pad_add_fusion.me_ref, f32[16,512]{1,0:T(8,128)} %pad_convert_fusion.gains, bf16[256,512]{1,0:T(8,128)(2,1)} %refs_0_.6, bf16[256,512]{1,0:T(8,128)(2,1)} %refs_1_.3, ...), custom_call_target="tpu_custom_call" | custom-call | flops 800000000 | bytes 1048576 | tf_op jit(solution)/shard_map/self_back/pallas_call | solution.py:399
  204.9 9.4 %self_back.3 = (f32[256,512]{1,0:T(8,128)}, f32[2,512]{1,0:T(2,128)}, bf16[2,2,4,2,32,512]{5,4,3,2,1,0:T(8,128)(2,1)}, bf16[2,2,4,2,32,512]{5,4,3,2,1,0:T(8,128)(2,1)}) custom-call(s32[4]{0:T(128)} %pad_add_fusion.me_ref, f32[16,512]{1,0:T(8,128)} %pad_convert_fusion.gains, bf16[256,512]{1,0:T(8,128)(2,1)} %refs_0_.7, ...), custom_call_target="tpu_custom_call" | custom-call | flops 400000000 | bytes 1048576 | tf_op jit(solution)/shard_map/self_back/pallas_call | solution.py:399
  215.5 1.8 collective-permute-done.34
  217.3 1.6 add_convert_fusion.4
  218.9 2.5 collective-permute-done.33
  226.1 1.6 collective-permute-start.50
  227.6 11.2 %collective-permute-done.50 = f32[16,512]{1,0:T(8,128)S(1)} collective-permute-done((f32[16,512]{1,0:T(8,128)S(1)}, f32[16,512]{1,0:T(8,128)S(1)}, u32[]{:S(2)}, u32[]{:S(2)}) %collective-permute-start.50) | collective-permute-done | bytes 32800 | tf_op jit(solution)/shard_map/ppermute | solution.py:551
  238.9 1.9 add_convert_fusion.6
  241.8 1.7 add_convert_fusion.3
  243.5 1.6 collective-permute-start.36
  245.1 2.5 add_convert_fusion
  248.9 2.3 add_convert_fusion.1
  252.9 2.0 collective-permute-start.37
  254.9 2.4 collective-permute-start.39
  262.8 1.8 collective-permute-done.38
  264.6 1.5 collective-permute-start.30
  266.4 1.6 collective-permute-start.54
  269.1 1.6 collective-permute-done.54
  274.5 19.1 %collective-permute-done.30 = bf16[2,4,2,64,512]{4,3,2,1,0:T(8,128)(2,1)} collective-permute-done((bf16[2,4,2,64,512]{4,3,2,1,0:T(8,128)(2,1)}, bf16[2,4,2,64,512]{4,3,2,1,0:T(8,128)(2,1)}, u32[]{:S(2)}, u32[]{:S(2)}) %collective-permute-start.30) | collective-permute-done | bytes 1048608 | tf_op jit(solution)/shard_map/ppermute | solution.py:559
  293.6 1.5 add_convert_fusion.7
  295.2 1.6 collective-permute-start.55
  296.7 1.9 add_convert_fusion.2
  299.3 5.1 %collective-permute-done.55 = bf16[4,2,64,512]{3,2,1,0:T(8,128)(2,1)S(1)} collective-permute-done((bf16[4,2,64,512]{3,2,1,0:T(8,128)(2,1)S(1)}, bf16[4,2,64,512]{3,2,1,0:T(8,128)(2,1)S(1)}, u32[]{:S(2)}, u32[]{:S(2)}) %collective-permute-start.55) | collective-permute-done | bytes 524320 | tf_op jit(solution)/shard_map/ppermute | solution.py:565
  305.2 3.2 collective-permute-start.58
  308.5 3.1 collective-permute-done.56
  312.9 2.9 collective-permute-done.57
  316.3 3.8 %collective-permute-start.46 = (bf16[2,96,512]{2,1,0:T(8,128)(2,1)S(1)}, bf16[2,96,512]{2,1,0:T(8,128)(2,1)S(1)}, u32[]{:S(2)}, u32[]{:S(2)}) collective-permute-start(bf16[2,96,512]{2,1,0:T(8,128)(2,1)S(1)} %get-tuple-element.134), channel_id=1, source_target_pairs={{0,12},{1,13},{2,14},{3,15},{4,0},{5,1},{6,2},{7,3},{8,4},{9,5},{1... | collective-permute-start | bytes 589832 | tf_op jit(solution)/shard_map/ppermute | solution.py:547
  322.2 1.6 collective-permute-start.60
  323.7 2.1 collective-permute-done.44
  325.8 2.0 collective-permute-done.46
  327.9 9.1 %collective-permute-done.45 = bf16[2,96,512]{2,1,0:T(8,128)(2,1)S(1)} collective-permute-done((bf16[2,96,512]{2,1,0:T(8,128)(2,1)S(1)}, bf16[2,96,512]{2,1,0:T(8,128)(2,1)S(1)}, u32[]{:S(2)}, u32[]{:S(2)}) %collective-permute-start.45) | collective-permute-done | bytes 196640 | tf_op jit(solution)/shard_map/ppermute | solution.py:547
  338.5 1.6 collective-permute-start.48
  341.5 4.0 %collective-permute-done.48 = bf16[2,96,512]{2,1,0:T(8,128)(2,1)S(1)} collective-permute-done((bf16[2,96,512]{2,1,0:T(8,128)(2,1)S(1)}, bf16[2,96,512]{2,1,0:T(8,128)(2,1)S(1)}, u32[]{:S(2)}, u32[]{:S(2)}) %collective-permute-start.48) | collective-permute-done | bytes 196640 | tf_op jit(solution)/shard_map/ppermute | solution.py:555
  (217 shorter events, 52.0 us)
Async XLA Ops:
  3.5 1.4 collective-permute-start
  5.0 8.9 %collective-permute-start.8 = (bf16[2,64,512]{2,1,0:T(8,128)(2,1)S(1)}, bf16[2,64,512]{2,1,0:T(8,128)(2,1)S(1)}, u32[]{:S(2)}, u32[]{:S(2)}) collective-permute-start(bf16[2,64,512]{2,1,0:T(8,128)(2,1)S(1)} %maximum_select_fusion.5), channel_id=1, source_target_pairs={{0,12},{1,13},{2,14},{3,15},{4,0},{5,1},{6,2},{7,3},{8,4},{9,5},{1... | collective-permute-start | bytes 393224 | tf_op jit(solution)/shard_map/ppermute | solution.py:547
  10.0 11.7 %collective-permute-start.7 = (bf16[2,64,512]{2,1,0:T(8,128)(2,1)S(1)}, bf16[2,64,512]{2,1,0:T(8,128)(2,1)S(1)}, u32[]{:S(2)}, u32[]{:S(2)}) collective-permute-start(bf16[2,64,512]{2,1,0:T(8,128)(2,1)S(1)} %maximum_select_fusion.5), channel_id=1, source_target_pairs={{0,8},{1,9},{2,10},{3,11},{4,12},{5,13},{6,14},{7,15},{8,0},{9,1},... | collective-permute-start | bytes 393224 | tf_op jit(solution)/shard_map/ppermute | solution.py:547
  10.0 11.7 %collective-permute-start.6 = (bf16[2,64,512]{2,1,0:T(8,128)(2,1)S(1)}, bf16[2,64,512]{2,1,0:T(8,128)(2,1)S(1)}, u32[]{:S(2)}, u32[]{:S(2)}) collective-permute-start(bf16[2,64,512]{2,1,0:T(8,128)(2,1)S(1)} %maximum_select_fusion.5), channel_id=1, source_target_pairs={{0,4},{1,5},{2,6},{3,7},{4,8},{5,9},{6,10},{7,11},{8,12},{9,13},{1... | collective-permute-start | bytes 393224 | tf_op jit(solution)/shard_map/ppermute | solution.py:547
  21.8 9.2 %collective-permute-start.9 = (bf16[4,2,64,512]{3,2,1,0:T(8,128)(2,1)S(1)}, bf16[4,2,64,512]{3,2,1,0:T(8,128)(2,1)S(1)}, u32[]{:S(2)}, u32[]{:S(2)}) collective-permute-start(bf16[4,2,64,512]{3,2,1,0:T(8,128)(2,1)S(1)} %get-tuple-element.149), channel_id=1, source_target_pairs={{0,16},{1,3},{2,18},{3,1},{4,20},{5,7},{6,22},{7,5},{8,24},{9,11},... | collective-permute-start | bytes 1572872 | tf_op jit(solution)/shard_map/ppermute | solution.py:565
  31.1 58.3 %copy-start.1 = (bf16[2,4,2,64,512]{4,3,2,1,0:T(8,128)(2,1)}, bf16[2,4,2,64,512]{4,3,2,1,0:T(8,128)(2,1)S(1)}, u32[]{:S(2)}) copy-start(bf16[2,4,2,64,512]{4,3,2,1,0:T(8,128)(2,1)S(1)} %pad_maximum_fusion.3.refs_2_.refs_1_.refs_7_.refs_6_) | copy-start | bytes 3145732
  31.2 23.9 %collective-permute-start.10 = (bf16[2,4,2,64,512]{4,3,2,1,0:T(8,128)(2,1)S(1)}, bf16[2,4,2,64,512]{4,3,2,1,0:T(8,128)(2,1)S(1)}, u32[]{:S(2)}, u32[]{:S(2)}) collective-permute-start(bf16[2,4,2,64,512]{4,3,2,1,0:T(8,128)(2,1)S(1)} %pad_maximum_fusion.3.refs_2_.refs_1_.refs_7_.refs_6_), channel_id=1, source_target_pairs={{0,2},{1,17},{2,0},{3,19},{4,6},{5,21},{6,4},{7,23},{8,10},{9,25},... | collective-permute-start | bytes 3145736 | tf_op jit(solution)/shard_map/ppermute | solution.py:559
  33.2 1.4 collective-permute-start.13
  34.6 7.0 %collective-permute-start.16 = (bf16[2,96,512]{2,1,0:T(8,128)(2,1)S(1)}, bf16[2,96,512]{2,1,0:T(8,128)(2,1)S(1)}, u32[]{:S(2)}, u32[]{:S(2)}) collective-permute-start(bf16[2,96,512]{2,1,0:T(8,128)(2,1)S(1)} %maximum_select_fusion.3), channel_id=1, source_target_pairs={{0,12},{1,13},{2,14},{3,15},{4,0},{5,1},{6,2},{7,3},{8,4},{9,5},{1... | collective-permute-start | bytes 589832 | tf_op jit(solution)/shard_map/ppermute | solution.py:547
  36.0 18.9 %collective-permute-start.15 = (bf16[2,96,512]{2,1,0:T(8,128)(2,1)S(1)}, bf16[2,96,512]{2,1,0:T(8,128)(2,1)S(1)}, u32[]{:S(2)}, u32[]{:S(2)}) collective-permute-start(bf16[2,96,512]{2,1,0:T(8,128)(2,1)S(1)} %maximum_select_fusion.3), channel_id=1, source_target_pairs={{0,8},{1,9},{2,10},{3,11},{4,12},{5,13},{6,14},{7,15},{8,0},{9,1},... | collective-permute-start | bytes 589832 | tf_op jit(solution)/shard_map/ppermute | solution.py:547
  37.2 17.8 %collective-permute-start.14 = (bf16[2,96,512]{2,1,0:T(8,128)(2,1)S(1)}, bf16[2,96,512]{2,1,0:T(8,128)(2,1)S(1)}, u32[]{:S(2)}, u32[]{:S(2)}) collective-permute-start(bf16[2,96,512]{2,1,0:T(8,128)(2,1)S(1)} %maximum_select_fusion.3), channel_id=1, source_target_pairs={{0,4},{1,5},{2,6},{3,7},{4,8},{5,9},{6,10},{7,11},{8,12},{9,13},{1... | collective-permute-start | bytes 589832 | tf_op jit(solution)/shard_map/ppermute | solution.py:547
  55.1 12.1 %collective-permute-start.17 = (bf16[4,2,96,512]{3,2,1,0:T(8,128)(2,1)S(1)}, bf16[4,2,96,512]{3,2,1,0:T(8,128)(2,1)S(1)}, u32[]{:S(2)}, u32[]{:S(2)}) collective-permute-start(bf16[4,2,96,512]{3,2,1,0:T(8,128)(2,1)S(1)} %pad_maximum_fusion.6), channel_id=1, source_target_pairs={{0,16},{1,3},{2,18},{3,1},{4,20},{5,7},{6,22},{7,5},{8,24},{9,11},... | collective-permute-start | bytes 2359304 | tf_op jit(solution)/shard_map/ppermute | solution.py:565
  67.3 31.5 %copy-start = (bf16[2,4,2,96,512]{4,3,2,1,0:T(8,128)(2,1)}, bf16[2,4,2,96,512]{4,3,2,1,0:T(8,128)(2,1)S(1)}, u32[]{:S(2)}) copy-start(bf16[2,4,2,96,512]{4,3,2,1,0:T(8,128)(2,1)S(1)} %pad_maximum_fusion.refs_0_) | copy-start | bytes 4718596
  67.3 20.6 %collective-permute-start.18 = (bf16[2,4,2,96,512]{4,3,2,1,0:T(8,128)(2,1)S(1)}, bf16[2,4,2,96,512]{4,3,2,1,0:T(8,128)(2,1)}, u32[]{:S(2)}, u32[]{:S(2)}) collective-permute-start(bf16[2,4,2,96,512]{4,3,2,1,0:T(8,128)(2,1)S(1)} %pad_maximum_fusion.refs_0_), channel_id=1, source_target_pairs={{0,2},{1,17},{2,0},{3,19},{4,6},{5,21},{6,4},{7,23},{8,10},{9,25},... | collective-permute-start | bytes 4718600 | tf_op jit(solution)/shard_map/ppermute | solution.py:559
  68.0 30.6 %copy-start.23 = (bf16[2,32]{1,0:T(2,128)(2,1)S(1)}, bf16[2,32]{1,0:T(2,128)(2,1)}, u32[]{:S(2)}) copy-start(bf16[2,32]{1,0:T(2,128)(2,1)} %param.34) | copy-start | bytes 388
  68.1 1.3 collective-permute-start.21
  69.5 6.1 %collective-permute-start.24 = (bf16[2,64,512]{2,1,0:T(8,128)(2,1)S(1)}, bf16[2,64,512]{2,1,0:T(8,128)(2,1)S(1)}, u32[]{:S(2)}, u32[]{:S(2)}) collective-permute-start(bf16[2,64,512]{2,1,0:T(8,128)(2,1)S(1)} %maximum_select_fusion.7), channel_id=1, source_target_pairs={{0,12},{1,13},{2,14},{3,15},{4,0},{5,1},{6,2},{7,3},{8,4},{9,5},{1... | collective-permute-start | bytes 393224 | tf_op jit(solution)/shard_map/ppermute | solution.py:547
  69.5 13.8 %collective-permute-start.23 = (bf16[2,64,512]{2,1,0:T(8,128)(2,1)S(1)}, bf16[2,64,512]{2,1,0:T(8,128)(2,1)S(1)}, u32[]{:S(2)}, u32[]{:S(2)}) collective-permute-start(bf16[2,64,512]{2,1,0:T(8,128)(2,1)S(1)} %maximum_select_fusion.7), channel_id=1, source_target_pairs={{0,8},{1,9},{2,10},{3,11},{4,12},{5,13},{6,14},{7,15},{8,0},{9,1},... | collective-permute-start | bytes 393224 | tf_op jit(solution)/shard_map/ppermute | solution.py:547
  71.2 12.2 %collective-permute-start.22 = (bf16[2,64,512]{2,1,0:T(8,128)(2,1)S(1)}, bf16[2,64,512]{2,1,0:T(8,128)(2,1)S(1)}, u32[]{:S(2)}, u32[]{:S(2)}) collective-permute-start(bf16[2,64,512]{2,1,0:T(8,128)(2,1)S(1)} %maximum_select_fusion.7), channel_id=1, source_target_pairs={{0,4},{1,5},{2,6},{3,7},{4,8},{5,9},{6,10},{7,11},{8,12},{9,13},{1... | collective-permute-start | bytes 393224 | tf_op jit(solution)/shard_map/ppermute | solution.py:547
  87.9 9.2 %collective-permute-start.25 = (bf16[4,2,64,512]{3,2,1,0:T(8,128)(2,1)S(1)}, bf16[4,2,64,512]{3,2,1,0:T(8,128)(2,1)S(1)}, u32[]{:S(2)}, u32[]{:S(2)}) collective-permute-start(bf16[4,2,64,512]{3,2,1,0:T(8,128)(2,1)S(1)} %pad_maximum_fusion.8), channel_id=1, source_target_pairs={{0,16},{1,3},{2,18},{3,1},{4,20},{5,7},{6,22},{7,5},{8,24},{9,11},... | collective-permute-start | bytes 1572872 | tf_op jit(solution)/shard_map/ppermute | solution.py:565
  89.4 30.6 %collective-permute-start.11 = (bf16[2,4,2,64,512]{4,3,2,1,0:T(8,128)(2,1)S(1)}, bf16[2,4,2,64,512]{4,3,2,1,0:T(8,128)(2,1)}, u32[]{:S(2)}, u32[]{:S(2)}) collective-permute-start(bf16[2,4,2,64,512]{4,3,2,1,0:T(8,128)(2,1)S(1)} %pad_maximum_fusion.3.refs_2_.refs_1_.refs_7_.refs_6_), channel_id=1, source_target_pairs={{0,1},{1,0},{2,3},{3,2},{4,5},{5,4},{6,7},{7,6},{8,9},{9,8},{10,11... | collective-permute-start | bytes 3145736 | tf_op jit(solution)/shard_map/ppermute | solution.py:543
  98.2 22.4 %collective-permute-start.26 = (bf16[2,4,2,64,512]{4,3,2,1,0:T(8,128)(2,1)}, bf16[2,4,2,64,512]{4,3,2,1,0:T(8,128)(2,1)}, u32[]{:S(2)}, u32[]{:S(2)}) collective-permute-start(bf16[2,4,2,64,512]{4,3,2,1,0:T(8,128)(2,1)} %pad_maximum_fusion.4.refs_0_), channel_id=1, source_target_pairs={{0,2},{1,17},{2,0},{3,19},{4,6},{5,21},{6,4},{7,23},{8,10},{9,25},... | collective-permute-start | bytes 3145736 | tf_op jit(solution)/shard_map/ppermute | solution.py:559
  98.8 1.2 collective-permute-start.1
  98.9 39.7 %collective-permute-start.19 = (bf16[2,4,2,96,512]{4,3,2,1,0:T(8,128)(2,1)S(1)}, bf16[2,4,2,96,512]{4,3,2,1,0:T(8,128)(2,1)}, u32[]{:S(2)}, u32[]{:S(2)}) collective-permute-start(bf16[2,4,2,96,512]{4,3,2,1,0:T(8,128)(2,1)S(1)} %pad_maximum_fusion.refs_0_), channel_id=1, source_target_pairs={{0,1},{1,0},{2,3},{3,2},{4,5},{5,4},{6,7},{7,6},{8,9},{9,8},{10,11... | collective-permute-start | bytes 4718600 | tf_op jit(solution)/shard_map/ppermute | solution.py:543
  99.4 39.2 %collective-permute-start.20 = (bf16[2,4,2,96,512]{4,3,2,1,0:T(8,128)(2,1)}, bf16[2,4,2,96,512]{4,3,2,1,0:T(8,128)(2,1)}, u32[]{:S(2)}, u32[]{:S(2)}) collective-permute-start(bf16[2,4,2,96,512]{4,3,2,1,0:T(8,128)(2,1)} %collective-permute-done.18.refs_1_), channel_id=1, source_target_pairs={{0,1},{1,0},{2,3},{3,2},{4,5},{5,4},{6,7},{7,6},{8,9},{9,8},{10,11... | collective-permute-start | bytes 4718600 | tf_op jit(solution)/shard_map/ppermute | solution.py:543
  100.0 4.0 %collective-permute-start.4 = (bf16[2,16,512]{2,1,0:T(8,128)(2,1)S(1)}, bf16[2,16,512]{2,1,0:T(8,128)(2,1)S(1)}, u32[]{:S(2)}, u32[]{:S(2)}) collective-permute-start(bf16[2,16,512]{2,1,0:T(8,128)(2,1)S(1)} %maximum_select_fusion.11), channel_id=1, source_target_pairs={{0,12},{1,13},{2,14},{3,15},{4,0},{5,1},{6,2},{7,3},{8,4},{9,5},{1... | collective-permute-start | bytes 98312 | tf_op jit(solution)/shard_map/ppermute | solution.py:547
  104.0 4.8 %collective-permute-start.3 = (bf16[2,16,512]{2,1,0:T(8,128)(2,1)S(1)}, bf16[2,16,512]{2,1,0:T(8,128)(2,1)S(1)}, u32[]{:S(2)}, u32[]{:S(2)}) collective-permute-start(bf16[2,16,512]{2,1,0:T(8,128)(2,1)S(1)} %maximum_select_fusion.11), channel_id=1, source_target_pairs={{0,8},{1,9},{2,10},{3,11},{4,12},{5,13},{6,14},{7,15},{8,0},{9,1},... | collective-permute-start | bytes 98312 | tf_op jit(solution)/shard_map/ppermute | solution.py:547
  108.8 6.2 %collective-permute-start.2 = (bf16[2,16,512]{2,1,0:T(8,128)(2,1)S(1)}, bf16[2,16,512]{2,1,0:T(8,128)(2,1)S(1)}, u32[]{:S(2)}, u32[]{:S(2)}) collective-permute-start(bf16[2,16,512]{2,1,0:T(8,128)(2,1)S(1)} %maximum_select_fusion.11), channel_id=1, source_target_pairs={{0,4},{1,5},{2,6},{3,7},{4,8},{5,9},{6,10},{7,11},{8,12},{9,13},{1... | collective-permute-start | bytes 98312 | tf_op jit(solution)/shard_map/ppermute | solution.py:547
  115.0 5.0 %collective-permute-start.5 = (bf16[4,2,16,512]{3,2,1,0:T(8,128)(2,1)S(1)}, bf16[4,2,16,512]{3,2,1,0:T(8,128)(2,1)S(1)}, u32[]{:S(2)}, u32[]{:S(2)}) collective-permute-start(bf16[4,2,16,512]{3,2,1,0:T(8,128)(2,1)S(1)} %get-tuple-element.161), channel_id=1, source_target_pairs={{0,2},{1,3},{2,0},{3,1},{4,6},{5,7},{6,4},{7,5},{8,10},{9,11},{10,... | collective-permute-start | bytes 393224 | tf_op jit(solution)/shard_map/ppermute | solution.py:551
  120.0 4.4 %collective-permute-start.12 = (bf16[2,4,2,64,512]{4,3,2,1,0:T(8,128)(2,1)}, bf16[2,4,2,64,512]{4,3,2,1,0:T(8,128)(2,1)}, u32[]{:S(2)}, u32[]{:S(2)}) collective-permute-start(bf16[2,4,2,64,512]{4,3,2,1,0:T(8,128)(2,1)} %copy-done.2), channel_id=1, source_target_pairs={{0,1},{1,0},{2,3},{3,2},{4,5},{5,4},{6,7},{7,6},{8,9},{9,8},{10,11... | collective-permute-start | bytes 3145736 | tf_op jit(solution)/shard_map/ppermute | solution.py:543
  120.0 33.1 %collective-permute-start.27 = (bf16[2,4,2,64,512]{4,3,2,1,0:T(8,128)(2,1)}, bf16[2,4,2,64,512]{4,3,2,1,0:T(8,128)(2,1)S(1)}, u32[]{:S(2)}, u32[]{:S(2)}) collective-permute-start(bf16[2,4,2,64,512]{4,3,2,1,0:T(8,128)(2,1)} %pad_maximum_fusion.4.refs_0_), channel_id=1, source_target_pairs={{0,1},{1,0},{2,3},{3,2},{4,5},{5,4},{6,7},{7,6},{8,9},{9,8},{10,11... | collective-permute-start | bytes 3145736 | tf_op jit(solution)/shard_map/ppermute | solution.py:543
  120.6 32.6 %collective-permute-start.28 = (bf16[2,4,2,64,512]{4,3,2,1,0:T(8,128)(2,1)}, bf16[2,4,2,64,512]{4,3,2,1,0:T(8,128)(2,1)}, u32[]{:S(2)}, u32[]{:S(2)}) collective-permute-start(bf16[2,4,2,64,512]{4,3,2,1,0:T(8,128)(2,1)} %collective-permute-done.26.refs_1_), channel_id=1, source_target_pairs={{0,1},{1,0},{2,3},{3,2},{4,5},{5,4},{6,7},{7,6},{8,9},{9,8},{10,11... | collective-permute-start | bytes 3145736 | tf_op jit(solution)/shard_map/ppermute | solution.py:543
  214.3 3.0 collective-permute-start.34
  214.5 6.9 %collective-permute-start.33 = (bf16[2,2,4,2,32,512]{5,4,3,2,1,0:T(8,128)(2,1)S(1)}, bf16[2,2,4,2,32,512]{5,4,3,2,1,0:T(8,128)(2,1)S(1)}, u32[]{:S(2)}, u32[]{:S(2)}) collective-permute-start(bf16[2,2,4,2,32,512]{5,4,3,2,1,0:T(8,128)(2,1)S(1)} %copy-done.25), channel_id=1, source_target_pairs={{0,1},{1,0},{2,3},{3,2},{4,5},{5,4},{6,7},{7,6},{8,9},{9,8},{10,11... | collective-permute-start | bytes 3145736 | tf_op jit(solution)/shard_map/ppermute | solution.py:543
  214.9 24.0 %collective-permute-start.31 = (bf16[2,2,4,2,32,512]{5,4,3,2,1,0:T(8,128)(2,1)}, bf16[2,2,4,2,32,512]{5,4,3,2,1,0:T(8,128)(2,1)}, u32[]{:S(2)}, u32[]{:S(2)}) collective-permute-start(bf16[2,2,4,2,32,512]{5,4,3,2,1,0:T(8,128)(2,1)} %get-tuple-element.103), channel_id=1, source_target_pairs={{0,1},{1,0},{2,3},{3,2},{4,5},{5,4},{6,7},{7,6},{8,9},{9,8},{10,11... | collective-permute-start | bytes 3145736 | tf_op jit(solution)/shard_map/ppermute | solution.py:543
  215.0 30.1 %collective-permute-start.32 = (bf16[2,2,4,2,64,512]{5,4,3,2,1,0:T(8,128)(2,1)}, bf16[2,2,4,2,64,512]{5,4,3,2,1,0:T(8,128)(2,1)}, u32[]{:S(2)}, u32[]{:S(2)}) collective-permute-start(bf16[2,2,4,2,64,512]{5,4,3,2,1,0:T(8,128)(2,1)} %get-tuple-element.105), channel_id=1, source_target_pairs={{0,1},{1,0},{2,3},{3,2},{4,5},{5,4},{6,7},{7,6},{8,9},{9,8},{10,11... | collective-permute-start | bytes 6291464 | tf_op jit(solution)/shard_map/ppermute | solution.py:543
  215.4 32.2 %collective-permute-start.29 = (bf16[2,2,4,2,64,512]{5,4,3,2,1,0:T(8,128)(2,1)}, bf16[2,2,4,2,64,512]{5,4,3,2,1,0:T(8,128)(2,1)S(1)}, u32[]{:S(2)}, u32[]{:S(2)}) collective-permute-start(bf16[2,2,4,2,64,512]{5,4,3,2,1,0:T(8,128)(2,1)} %get-tuple-element.89), channel_id=1, source_target_pairs={{0,1},{1,0},{2,3},{3,2},{4,5},{5,4},{6,7},{7,6},{8,9},{9,8},{10,11... | collective-permute-start | bytes 6291464 | tf_op jit(solution)/shard_map/ppermute | solution.py:543
  223.1 18.6 %collective-permute-start.35 = (bf16[2,4,2,64,512]{4,3,2,1,0:T(8,128)(2,1)}, bf16[2,4,2,64,512]{4,3,2,1,0:T(8,128)(2,1)}, u32[]{:S(2)}, u32[]{:S(2)}) collective-permute-start(bf16[2,4,2,64,512]{4,3,2,1,0:T(8,128)(2,1)} %pad_maximum_fusion.5), channel_id=1, source_target_pairs={{0,2},{1,17},{2,0},{3,19},{4,6},{5,21},{6,4},{7,23},{8,10},{9,25},... | collective-permute-start | bytes 3145736 | tf_op jit(solution)/shard_map/ppermute | solution.py:559
  224.7 1.3 collective-permute-start.49
  226.1 12.8 %collective-permute-start.50 = (f32[16,512]{1,0:T(8,128)S(1)}, f32[16,512]{1,0:T(8,128)S(1)}, u32[]{:S(2)}, u32[]{:S(2)}) collective-permute-start(f32[16,512]{1,0:T(8,128)S(1)} %pad_add_fusion.1), channel_id=1, source_target_pairs={{0,2},{1,3},{2,0},{3,1},{4,6},{5,7},{6,4},{7,5},{8,10},{9,11},{10,... | collective-permute-start | bytes 98312 | tf_op jit(solution)/shard_map/ppermute | solution.py:551
  238.9 27.4 %collective-permute-start.53 = (f32[16,512]{1,0:T(8,128)S(1)}, f32[16,512]{1,0:T(8,128)S(1)}, u32[]{:S(2)}, u32[]{:S(2)}) collective-permute-start(f32[16,512]{1,0:T(8,128)S(1)} %add.121), channel_id=1, source_target_pairs={{0,12},{1,13},{2,14},{3,15},{4,0},{5,1},{6,2},{7,3},{8,4},{9,5},{1... | collective-permute-start | bytes 98312 | tf_op jit(solution)/shard_map/ppermute | solution.py:547
  238.9 27.5 %collective-permute-start.52 = (f32[16,512]{1,0:T(8,128)S(1)}, f32[16,512]{1,0:T(8,128)S(1)}, u32[]{:S(2)}, u32[]{:S(2)}) collective-permute-start(f32[16,512]{1,0:T(8,128)S(1)} %add.121), channel_id=1, source_target_pairs={{0,8},{1,9},{2,10},{3,11},{4,12},{5,13},{6,14},{7,15},{8,0},{9,1},... | collective-permute-start | bytes 98312 | tf_op jit(solution)/shard_map/ppermute | solution.py:547
  243.5 9.2 %collective-permute-start.36 = (bf16[4,2,64,512]{3,2,1,0:T(8,128)(2,1)S(1)}, bf16[4,2,64,512]{3,2,1,0:T(8,128)(2,1)S(1)}, u32[]{:S(2)}, u32[]{:S(2)}) collective-permute-start(bf16[4,2,64,512]{3,2,1,0:T(8,128)(2,1)S(1)} %slice_bitcast_fusion.8), channel_id=1, source_target_pairs={{0,16},{1,3},{2,18},{3,1},{4,20},{5,7},{6,22},{7,5},{8,24},{9,11},... | collective-permute-start | bytes 1572872 | tf_op jit(solution)/shard_map/ppermute | solution.py:565
  252.9 7.4 %collective-permute-start.37 = (bf16[2,64,512]{2,1,0:T(8,128)(2,1)S(1)}, bf16[2,64,512]{2,1,0:T(8,128)(2,1)S(1)}, u32[]{:S(2)}, u32[]{:S(2)}) collective-permute-start(bf16[2,64,512]{2,1,0:T(8,128)(2,1)S(1)} %get-tuple-element.145), channel_id=1, source_target_pairs={{0,4},{1,5},{2,6},{3,7},{4,8},{5,9},{6,10},{7,11},{8,12},{9,13},{1... | collective-permute-start | bytes 393224 | tf_op jit(solution)/shard_map/ppermute | solution.py:547
  254.9 6.7 %collective-permute-start.39 = (bf16[2,64,512]{2,1,0:T(8,128)(2,1)S(1)}, bf16[2,64,512]{2,1,0:T(8,128)(2,1)S(1)}, u32[]{:S(2)}, u32[]{:S(2)}) collective-permute-start(bf16[2,64,512]{2,1,0:T(8,128)(2,1)S(1)} %get-tuple-element.146), channel_id=1, source_target_pairs={{0,12},{1,13},{2,14},{3,15},{4,0},{5,1},{6,2},{7,3},{8,4},{9,5},{1... | collective-permute-start | bytes 393224 | tf_op jit(solution)/shard_map/ppermute | solution.py:547
  257.4 7.3 %collective-permute-start.38 = (bf16[2,64,512]{2,1,0:T(8,128)(2,1)S(1)}, bf16[2,64,512]{2,1,0:T(8,128)(2,1)S(1)}, u32[]{:S(2)}, u32[]{:S(2)}) collective-permute-start(bf16[2,64,512]{2,1,0:T(8,128)(2,1)S(1)} %get-tuple-element.147), channel_id=1, source_target_pairs={{0,8},{1,9},{2,10},{3,11},{4,12},{5,13},{6,14},{7,15},{8,0},{9,1},... | collective-permute-start | bytes 393224 | tf_op jit(solution)/shard_map/ppermute | solution.py:547
  260.4 6.0 %collective-permute-start.51 = (f32[16,512]{1,0:T(8,128)S(1)}, f32[16,512]{1,0:T(8,128)S(1)}, u32[]{:S(2)}, u32[]{:S(2)}) collective-permute-start(f32[16,512]{1,0:T(8,128)S(1)} %add.121), channel_id=1, source_target_pairs={{0,4},{1,5},{2,6},{3,7},{4,8},{5,9},{6,10},{7,11},{8,12},{9,13},{1... | collective-permute-start | bytes 98312 | tf_op jit(solution)/shard_map/ppermute | solution.py:547
  261.6 35.1 %collective-permute-start.42 = (bf16[2,4,2,96,512]{4,3,2,1,0:T(8,128)(2,1)}, bf16[2,4,2,96,512]{4,3,2,1,0:T(8,128)(2,1)}, u32[]{:S(2)}, u32[]{:S(2)}) collective-permute-start(bf16[2,4,2,96,512]{4,3,2,1,0:T(8,128)(2,1)} %pad_maximum_fusion.2), channel_id=1, source_target_pairs={{0,2},{1,17},{2,0},{3,19},{4,6},{5,21},{6,4},{7,23},{8,10},{9,25},... | collective-permute-start | bytes 4718600 | tf_op jit(solution)/shard_map/ppermute | solution.py:559
  264.6 29.0 %collective-permute-start.30 = (bf16[2,4,2,64,512]{4,3,2,1,0:T(8,128)(2,1)}, bf16[2,4,2,64,512]{4,3,2,1,0:T(8,128)(2,1)}, u32[]{:S(2)}, u32[]{:S(2)}) collective-permute-start(bf16[2,4,2,64,512]{4,3,2,1,0:T(8,128)(2,1)} %slice_bitcast_fusion.2), channel_id=1, source_target_pairs={{0,2},{1,17},{2,0},{3,19},{4,6},{5,21},{6,4},{7,23},{8,10},{9,25},... | collective-permute-start | bytes 3145736 | tf_op jit(solution)/shard_map/ppermute | solution.py:559
  266.3 1.7 collective-permute-start.40
  266.4 4.4 %collective-permute-start.54 = (f32[16,512]{1,0:T(8,128)S(1)}, f32[16,512]{1,0:T(8,128)S(1)}, u32[]{:S(2)}, u32[]{:S(2)}) collective-permute-start(f32[16,512]{1,0:T(8,128)S(1)} %add_add_fusion), channel_id=1, source_target_pairs={{0,16},{1,17},{2,18},{3,19},{4,20},{5,21},{6,22},{7,23},{8,24},{9,... | collective-permute-start | bytes 98312 | tf_op jit(solution)/shard_map/ppermute | solution.py:555
  267.9 6.5 %collective-permute-start.41 = (bf16[2,64,512]{2,1,0:T(8,128)(2,1)S(1)}, bf16[2,64,512]{2,1,0:T(8,128)(2,1)S(1)}, u32[]{:S(2)}, u32[]{:S(2)}) collective-permute-start(bf16[2,64,512]{2,1,0:T(8,128)(2,1)S(1)} %maximum_select_fusion.8), channel_id=1, source_target_pairs={{0,16},{1,17},{2,18},{3,19},{4,20},{5,21},{6,22},{7,23},{8,24},{9,... | collective-permute-start | bytes 393224 | tf_op jit(solution)/shard_map/ppermute | solution.py:555
  295.2 9.2 %collective-permute-start.55 = (bf16[4,2,64,512]{3,2,1,0:T(8,128)(2,1)S(1)}, bf16[4,2,64,512]{3,2,1,0:T(8,128)(2,1)S(1)}, u32[]{:S(2)}, u32[]{:S(2)}) collective-permute-start(bf16[4,2,64,512]{3,2,1,0:T(8,128)(2,1)S(1)} %slice_bitcast_fusion.6), channel_id=1, source_target_pairs={{0,16},{1,3},{2,18},{3,1},{4,20},{5,7},{6,22},{7,5},{8,24},{9,11},... | collective-permute-start | bytes 1572872 | tf_op jit(solution)/shard_map/ppermute | solution.py:565
  298.7 17.3 %collective-permute-start.43 = (bf16[4,2,96,512]{3,2,1,0:T(8,128)(2,1)S(1)}, bf16[4,2,96,512]{3,2,1,0:T(8,128)(2,1)S(1)}, u32[]{:S(2)}, u32[]{:S(2)}) collective-permute-start(bf16[4,2,96,512]{3,2,1,0:T(8,128)(2,1)S(1)} %slice_bitcast_fusion.4), channel_id=1, source_target_pairs={{0,16},{1,3},{2,18},{3,1},{4,20},{5,7},{6,22},{7,5},{8,24},{9,11},... | collective-permute-start | bytes 2359304 | tf_op jit(solution)/shard_map/ppermute | solution.py:565
  304.6 7.0 %collective-permute-start.56 = (bf16[2,64,512]{2,1,0:T(8,128)(2,1)S(1)}, bf16[2,64,512]{2,1,0:T(8,128)(2,1)S(1)}, u32[]{:S(2)}, u32[]{:S(2)}) collective-permute-start(bf16[2,64,512]{2,1,0:T(8,128)(2,1)S(1)} %get-tuple-element.138), channel_id=1, source_target_pairs={{0,4},{1,5},{2,6},{3,7},{4,8},{5,9},{6,10},{7,11},{8,12},{9,13},{1... | collective-permute-start | bytes 393224 | tf_op jit(solution)/shard_map/ppermute | solution.py:547
  305.2 7.6 %collective-permute-start.58 = (bf16[2,64,512]{2,1,0:T(8,128)(2,1)S(1)}, bf16[2,64,512]{2,1,0:T(8,128)(2,1)S(1)}, u32[]{:S(2)}, u32[]{:S(2)}) collective-permute-start(bf16[2,64,512]{2,1,0:T(8,128)(2,1)S(1)} %get-tuple-element.139), channel_id=1, source_target_pairs={{0,12},{1,13},{2,14},{3,15},{4,0},{5,1},{6,2},{7,3},{8,4},{9,5},{1... | collective-permute-start | bytes 393224 | tf_op jit(solution)/shard_map/ppermute | solution.py:547
  308.5 7.3 %collective-permute-start.57 = (bf16[2,64,512]{2,1,0:T(8,128)(2,1)S(1)}, bf16[2,64,512]{2,1,0:T(8,128)(2,1)S(1)}, u32[]{:S(2)}, u32[]{:S(2)}) collective-permute-start(bf16[2,64,512]{2,1,0:T(8,128)(2,1)S(1)} %get-tuple-element.140), channel_id=1, source_target_pairs={{0,8},{1,9},{2,10},{3,11},{4,12},{5,13},{6,14},{7,15},{8,0},{9,1},... | collective-permute-start | bytes 393224 | tf_op jit(solution)/shard_map/ppermute | solution.py:547
  315.9 6.3 %collective-permute-start.59 = (bf16[64,512]{1,0:T(8,128)(2,1)S(1)}, bf16[64,512]{1,0:T(8,128)(2,1)S(1)}, u32[]{:S(2)}, u32[]{:S(2)}) collective-permute-start(bf16[64,512]{1,0:T(8,128)(2,1)S(1)} %get-tuple-element.157), channel_id=1, source_target_pairs={{0,1},{1,0},{2,3},{3,2},{4,5},{5,4},{6,7},{7,6},{8,9},{9,8},{10,11... | collective-permute-start | bytes 196616 | tf_op jit(solution)/shard_map/ppermute | solution.py:543
  316.2 9.6 %collective-permute-start.44 = (bf16[2,96,512]{2,1,0:T(8,128)(2,1)S(1)}, bf16[2,96,512]{2,1,0:T(8,128)(2,1)S(1)}, u32[]{:S(2)}, u32[]{:S(2)}) collective-permute-start(bf16[2,96,512]{2,1,0:T(8,128)(2,1)S(1)} %get-tuple-element.133), channel_id=1, source_target_pairs={{0,4},{1,5},{2,6},{3,7},{4,8},{5,9},{6,10},{7,11},{8,12},{9,13},{1... | collective-permute-start | bytes 589832 | tf_op jit(solution)/shard_map/ppermute | solution.py:547
  316.3 11.6 %collective-permute-start.46 = (bf16[2,96,512]{2,1,0:T(8,128)(2,1)S(1)}, bf16[2,96,512]{2,1,0:T(8,128)(2,1)S(1)}, u32[]{:S(2)}, u32[]{:S(2)}) collective-permute-start(bf16[2,96,512]{2,1,0:T(8,128)(2,1)S(1)} %get-tuple-element.134), channel_id=1, source_target_pairs={{0,12},{1,13},{2,14},{3,15},{4,0},{5,1},{6,2},{7,3},{8,4},{9,5},{1... | collective-permute-start | bytes 589832 | tf_op jit(solution)/shard_map/ppermute | solution.py:547
  320.1 16.9 %collective-permute-start.45 = (bf16[2,96,512]{2,1,0:T(8,128)(2,1)S(1)}, bf16[2,96,512]{2,1,0:T(8,128)(2,1)S(1)}, u32[]{:S(2)}, u32[]{:S(2)}) collective-permute-start(bf16[2,96,512]{2,1,0:T(8,128)(2,1)S(1)} %get-tuple-element.135), channel_id=1, source_target_pairs={{0,8},{1,9},{2,10},{3,11},{4,12},{5,13},{6,14},{7,15},{8,0},{9,1},... | collective-permute-start | bytes 589832 | tf_op jit(solution)/shard_map/ppermute | solution.py:547
  322.2 15.0 %collective-permute-start.60 = (bf16[2,64,512]{2,1,0:T(8,128)(2,1)S(1)}, bf16[2,64,512]{2,1,0:T(8,128)(2,1)S(1)}, u32[]{:S(2)}, u32[]{:S(2)}) collective-permute-start(bf16[2,64,512]{2,1,0:T(8,128)(2,1)S(1)} %maximum_select_fusion.9), channel_id=1, source_target_pairs={{0,16},{1,17},{2,18},{3,19},{4,20},{5,21},{6,22},{7,23},{8,24},{9,... | collective-permute-start | bytes 393224 | tf_op jit(solution)/shard_map/ppermute | solution.py:555
  337.1 1.4 collective-permute-start.47
  338.5 7.0 %collective-permute-start.48 = (bf16[2,96,512]{2,1,0:T(8,128)(2,1)S(1)}, bf16[2,96,512]{2,1,0:T(8,128)(2,1)S(1)}, u32[]{:S(2)}, u32[]{:S(2)}) collective-permute-start(bf16[2,96,512]{2,1,0:T(8,128)(2,1)S(1)} %maximum_select_fusion.4), channel_id=1, source_target_pairs={{0,16},{1,17},{2,18},{3,19},{4,20},{5,21},{6,22},{7,23},{8,24},{9,... | collective-permute-start | bytes 589832 | tf_op jit(solution)/shard_map/ppermute | solution.py:555
  (23 other events, 275.3 us)
